TPU v7x, 128 devices: a whole 4x4x4 slice. The times are simulated.
128 devices in a mesh: lon: 32 (over x, z, y_hi), lat: 4 (over y_lo, core).
Axes of the slice: x: 4, y: 4 (y_hi: 2, y_lo: 2; y = y_hi * 2 + y_lo), z: 4, core: 2. Of those that a mesh axis runs over, the one named last changes fastest.
Arguments:
- tokens: bfloat16 [2, 48, 384, 512], P(None, 'lat', 'lon'), may hold values from -6 to 6
- cotangent: bfloat16 [2, 48, 384, 512], P(None, 'lat', 'lon'), may hold values from -6 to 6
- gain_first: float32 [512], replicated, may hold values from 0.5 to 1.5
- gain_second: float32 [512], replicated, may hold values from 0.5 to 1.5
- qkv_first: bfloat16 [512, 1536], replicated, may hold values from -0.25 to 0.25
- qkv_second: bfloat16 [512, 1536], replicated, may hold values from -0.25 to 0.25
- proj_first: bfloat16 [512, 512], replicated, may hold values from -0.25 to 0.25
- proj_second: bfloat16 [512, 512], replicated, may hold values from -0.25 to 0.25
- table_first: float32 [16, 1587], replicated, may hold values from -6 to 250
- table_second: float32 [16, 1587], replicated, may hold values from -6 to 250
- rel_index: int32 [288, 288], replicated, may hold values from 0 to 1586
- regions: int32 [2, 48, 384], P(None, 'lat', 'lon'), may hold values from 0 to 3, as said below
Outputs:
- mixed: bfloat16 [2, 48, 384, 512], P(None, 'lat', 'lon')
- grad_tokens: bfloat16 [2, 48, 384, 512], P(None, 'lat', 'lon')
- grad_gain_first: float32 [512], replicated
- grad_gain_second: float32 [512], replicated
- grad_qkv_first: float32 [512, 1536], replicated
- grad_qkv_second: float32 [512, 1536], replicated
- grad_proj_first: float32 [512, 512], replicated
- grad_proj_second: float32 [512, 512], replicated
- grad_table_first: float32 [16, 1587], replicated
- grad_table_second: float32 [16, 1587], replicated
Inputs may be any that keep to these rules, and one draw needn't show every extreme that they name: `regions`: within each window of 12 patch rows and 12 patch columns (all levels), either all patches carry one id, or the last 6 patch rows of the window carry one id and its other patches a different id; windows holding the grid's last 6 patch rows are always split this way. Which windows are split, and the ids, are drawn anew for every window.
All inputs are finite; a program needn't handle non-finite values.
Results may differ from a plain program's by a relative error of at most 0.019.
Values may be sent and summed in bfloat16 or wider, within the bound.
A program may use at most 192 MiB of HBM per device.

v0:
```python
import jax
import jax.numpy as jnp
from jax import lax
from jax.sharding import PartitionSpec as P

WIN = 12
HALF = 6


EPS = 1e-05


def passed_along(array, axis, by):
    count = lax.axis_size(axis)
    return lax.ppermute(array, axis, [(i, (i + by) % count) for i in range(count)])


def norm_rows(values, gain):
    center = jnp.mean(values, -1, keepdims=True)
    centred = values - center
    spread = jnp.mean(centred * centred, -1, keepdims=True)
    return (centred * lax.rsqrt(spread + EPS) * gain).astype(jnp.bfloat16)


def to_windows(grid):
    levels, rows, cols, width = grid.shape
    parts = grid.reshape(levels, rows // WIN, WIN, cols // WIN, WIN, width)
    parts = parts.transpose(1, 3, 0, 2, 4, 5)
    return parts.reshape(-1, levels * WIN * WIN, width)


def from_windows(blocks, levels, rows, cols):
    width = blocks.shape[-1]
    parts = blocks.reshape(rows // WIN, cols // WIN, levels, WIN, WIN, width)
    return parts.transpose(2, 0, 3, 1, 4, 5).reshape(levels, rows, cols, width)


def window_attention(packed, labels, bias):
    heads = bias.shape[0]
    width = packed.shape[1] // 3
    depth = width // heads
    number = packed.shape[0]
    query = packed[:, :width].reshape(number, heads, depth)
    keyset = packed[:, width : 2 * width].reshape(number, heads, depth)
    valueset = packed[:, 2 * width :].reshape(number, heads, depth)
    scores = (
        jnp.einsum("qhd,khd->hqk", query, keyset, preferred_element_type=jnp.float32)
        * depth ** (-0.5)
        + bias
    )
    allowed = labels[:, None] == labels[None, :]
    scores = jnp.where(allowed[None], scores, -1e30)
    highest = jnp.max(scores, -1, keepdims=True)
    expo = jnp.exp(scores - highest)
    weights = (expo / jnp.sum(expo, -1, keepdims=True)).astype(jnp.bfloat16)
    context = jnp.einsum("hqk,khd->qhd", weights, valueset, preferred_element_type=jnp.float32)
    return context.reshape(number, width).astype(jnp.bfloat16)


def attend(projected, table, rel_index, labels):
    bias = table[:, rel_index]
    levels, rows, cols, _ = projected.shape
    blocks = to_windows(projected)
    marks = to_windows(labels[..., None])[..., 0]
    result = jax.vmap(window_attention, in_axes=(0, 0, None))(blocks, marks, bias)
    return from_windows(result, levels, rows, cols)


def block_forward(inputs, gain, qkv_weight, proj_weight, table, rel_index, labels):
    widened = inputs.astype(jnp.float32)
    normed = norm_rows(widened, gain)
    projected = jnp.dot(normed, qkv_weight, preferred_element_type=jnp.float32).astype(jnp.bfloat16)
    context = attend(projected, table, rel_index, labels)
    output = (widened + jnp.dot(context, proj_weight, preferred_element_type=jnp.float32)).astype(
        jnp.bfloat16
    )
    return (output, (normed, projected, context))


def block_backward(
    grad_out, inputs, saved, gain, qkv_weight, proj_weight, table, rel_index, labels
):
    normed, projected, context = saved
    width = inputs.shape[-1]
    grad_proj = lax.dot_general(
        context.reshape(-1, width),
        grad_out.reshape(-1, width),
        (((0,), (0,)), ((), ())),
        preferred_element_type=jnp.float32,
    )
    grad_context = jnp.dot(grad_out, proj_weight.T, preferred_element_type=jnp.float32).astype(
        jnp.bfloat16
    )
    _, pull = jax.vjp(lambda p, t: attend(p, t, rel_index, labels), projected, table)
    grad_projected, grad_table = pull(grad_context)
    grad_qkv = lax.dot_general(
        normed.reshape(-1, width),
        grad_projected.reshape(-1, 3 * width),
        (((0,), (0,)), ((), ())),
        preferred_element_type=jnp.float32,
    )
    grad_normed = jnp.dot(grad_projected, qkv_weight.T, preferred_element_type=jnp.float32).astype(
        jnp.bfloat16
    )
    _, pull_norm = jax.vjp(norm_rows, inputs.astype(jnp.float32), gain)
    grad_widened, grad_gain = pull_norm(grad_normed)
    grad_inputs = (grad_widened + grad_out.astype(jnp.float32)).astype(jnp.bfloat16)
    return (grad_inputs, (grad_gain, grad_qkv, grad_proj, grad_table))


def on_device(
    tokens,
    cotangent,
    gain_first,
    gain_second,
    qkv_first,
    qkv_second,
    proj_first,
    proj_second,
    table_first,
    table_second,
    rel_index,
    regions,
):
    plain = jnp.zeros(tokens.shape[:3], jnp.int32)
    first_out, first_saved = block_forward(
        tokens, gain_first, qkv_first, proj_first, table_first, rel_index, plain
    )
    strip = passed_along(first_out[:, :, :HALF], "lon", -1)
    widened = jnp.concatenate([first_out[:, :, HALF:], strip], 2)
    edge = passed_along(widened[:, :HALF], "lat", -1)
    shifted = jnp.concatenate([widened[:, HALF:], edge], 1)
    mixed, second_saved = block_forward(
        shifted, gain_second, qkv_second, proj_second, table_second, rel_index, regions
    )
    grad_shifted, second_grads = block_backward(
        cotangent,
        shifted,
        second_saved,
        gain_second,
        qkv_second,
        proj_second,
        table_second,
        rel_index,
        regions,
    )
    back_strip = passed_along(grad_shifted[:, :, -HALF:], "lon", 1)
    back_wide = jnp.concatenate([back_strip, grad_shifted[:, :, :-HALF]], 2)
    back_edge = passed_along(back_wide[:, -HALF:], "lat", 1)
    grad_first_out = jnp.concatenate([back_edge, back_wide[:, :-HALF]], 1)
    grad_tokens, first_grads = block_backward(
        grad_first_out,
        tokens,
        first_saved,
        gain_first,
        qkv_first,
        proj_first,
        table_first,
        rel_index,
        plain,
    )
    summed = lax.psum(
        (
            first_grads[0],
            first_grads[1],
            first_grads[2],
            first_grads[3],
            second_grads[0],
            second_grads[1],
            second_grads[2],
            second_grads[3],
        ),
        ("lon", "lat"),
    )
    first_grads = summed[:4]
    second_grads = summed[4:]
    return (
        mixed,
        grad_tokens,
        first_grads[0],
        second_grads[0],
        first_grads[1],
        second_grads[1],
        first_grads[2],
        second_grads[2],
        first_grads[3],
        second_grads[3],
    )


def solution(mesh):
    return jax.shard_map(
        on_device,
        mesh=mesh,
        in_specs=(
            P(None, "lat", "lon", None),
            P(None, "lat", "lon", None),
            P(),
            P(),
            P(),
            P(),
            P(),
            P(),
            P(),
            P(),
            P(),
            P(None, "lat", "lon"),
        ),
        out_specs=(
            P(None, "lat", "lon", None),
            P(None, "lat", "lon", None),
            P(),
            P(),
            P(),
            P(),
            P(),
            P(),
            P(),
            P(),
        ),
        check_vma=False,
    )
```

profile of v0, /device:TPU:1, one launch (start us, length us, event | category | flops | bytes accessed | tf_op | source)
XLA Modules:
  0.0 1901.4 jit_solution(11714719430209080726)
XLA Ops:
  13.7 3.4 convolution_convert_fusion.1
  17.1 2.1 reshape_transpose_reshape.8
  19.2 2.1 fusion.115
  22.5 2.0 copy.53
  24.5 1.9 copy.52
  26.4 274.5 %gather_fusion = f32[82944,16]{1,0:T(8,128)} fusion(f32[16,1587]{0,1:T(8,128)S(1)} %copy.55, s32[82944]{0:T(1024)S(1)} %broadcast_clamp_fusion), kind=kCustom, calls=%fused_computation | custom fusion | bytes 10948608 | tf_op jit(solution)/shard_map/gather | solution.py:61
  300.9 29.5 %copy.57 = f32[288,288,16]{0,1,2:T(8,128)} copy(f32[288,288,16]{2,1,0:T(8,128)} %bitcast.151) | data formatting | bytes 10616832 | tf_op jit(solution)/shard_map/gather | solution.py:61
  330.4 4.2 fusion.118
  335.7 4.1 convert_reduce_fusion
  343.1 2.1 copy.59
  345.2 1.9 convert_element_type.213
  349.3 9.6 collective-permute-start
  360.0 2.3 convolution_convert_fusion.7
  363.1 1.8 reshape.507
  364.9 1.8 copy.70
  367.0 274.5 %gather_fusion.1 = f32[82944,16]{1,0:T(8,128)} fusion(f32[16,1587]{0,1:T(8,128)S(1)} %copy.64, s32[82944]{0:T(1024)S(1)} %broadcast_clamp_fusion), kind=kCustom, calls=%fused_computation.1 | custom fusion | bytes 10948608 | tf_op jit(solution)/shard_map/gather | solution.py:61
  641.5 29.5 %copy.66 = f32[288,288,16]{0,1,2:T(8,128)} copy(f32[288,288,16]{2,1,0:T(8,128)} %bitcast.150) | data formatting | bytes 10616832 | tf_op jit(solution)/shard_map/gather | solution.py:61
  674.5 3.5 collective-permute-done.1
  685.5 5.0 fusion.119
  690.5 2.9 copy-done.2
  694.7 6.1 convert_reduce_fusion.1
  700.9 3.0 fusion.112
  705.8 2.8 fusion.58
  708.6 2.6 fusion.55
  711.2 4.0 fusion.28
  716.4 1.9 copy.75
  720.5 2.2 fusion.84
  727.4 2.7 fusion.73
  730.1 27.7 %copy.113 = f32[288,288,16]{2,1,0:T(8,128)} copy(f32[288,288,16]{0,1,2:T(8,128)} %fusion.28) | data formatting | bytes 10616832 | tf_op jit(solution)/shard_map/transpose(jvp(vmap(jit(_where))))/select_n | solution.py:52
  757.8 440.3 %scatter_custom_fusion.1 = f32[16,1587]{0,1:T(8,128)} fusion(s32[82944]{0:T(1024)} %copy-done.20, f32[82944,16]{1,0:T(8,128)} %bitcast.153, f32[]{:T(128)} %constant.12.clone.1), kind=kCustom, calls=%fused_computation.116 | custom fusion | flops 1327104 | bytes 102080 | tf_op jit(solution)/shard_map/transpose(jvp())/scatter-add | solution.py:61
  1206.6 1.8 copy.79
  1208.4 4.1 convolution_convert_fusion.4
  1212.5 5.3 fusion.7
  1217.9 2.2 fusion.110
  1223.2 3.9 fusion.19
  1227.0 1.9 copy.81
  1233.1 2.7 fusion.82
  1238.3 1.9 fusion.79
  1240.2 3.7 fusion.75
  1244.0 27.4 %copy.112 = f32[288,288,16]{2,1,0:T(8,128)} copy(f32[288,288,16]{0,1,2:T(8,128)} %fusion.19) | data formatting | bytes 10616832 | tf_op jit(solution)/shard_map/transpose(jvp(vmap()))/add_any | solution.py:53
  1271.4 440.5 %scatter_custom_fusion = f32[16,1587]{0,1:T(8,128)} fusion(s32[82944]{0:T(1024)} %copy-done.20, f32[82944,16]{1,0:T(8,128)} %bitcast.152, f32[]{:T(128)} %constant.12.clone.1), kind=kCustom, calls=%fused_computation.118 | custom fusion | flops 1327104 | bytes 102080 | tf_op jit(solution)/shard_map/transpose(jvp())/scatter-add | solution.py:61
  1713.4 2.1 copy.68
  1715.5 1.9 convert_element_type.222
  1721.0 67.3 %all-reduce.6 = (f32[512]{0:T(512)}, f32[512]{0:T(512)}) all-reduce(f32[512]{0:T(512)S(1)} %copy-done.50, f32[512]{0:T(512)S(1)} %copy-done.49), channel_id=1, replica_groups=mesh['lon'=32,'lat'=4] {'lon','lat'}, use_global_device_ids=true, to_apply=%region_19.20 | all-reduce | flops 1024 | bytes 8192 | tf_op jit(solution)/shard_map/psum | solution.py:162
  1788.3 94.3 %all-reduce.10.cloned.1.call-done = (f32[512,1536]{1,0:T(8,128)}, f32[512,1536]{1,0:T(8,128)}, f32[512,512]{1,0:T(8,128)}, f32[512,512]{1,0:T(8,128)}, f32[16,1587]{0,1:T(8,128)}, /*index=5*/f32[16,1587]{0,1:T(8,128)}) async-done(((f32[512,1536]{1,0:T(8,128)}, f32[512,1536]{1,0:T(8,128)}, f32[512,512]{1,0:T(8,128)}, f32[512,512]{1,0:T(8,128)}, f32[16,1587]{0,1:T(8,128)}, /*index=5*/f32[16,1587]{0,1:T(8,128)}), ...) | async-done | bytes 8591760 | tf_op jit(solution)/shard_map/psum | solution.py:162
  1882.6 2.1 copy.94
  1884.7 2.1 copy.95
  1886.8 3.9 copy.145
  (187 shorter events, 65.1 us)
Async XLA Ops:
  7.2 672.9 %copy-start = (bf16[512,1536]{1,0:T(8,128)(2,1)S(1)}, bf16[512,1536]{1,0:T(8,128)(2,1)}, u32[]{:S(2)}) copy-start(bf16[512,1536]{1,0:T(8,128)(2,1)} %param.17) | copy-start | bytes 4718596
  7.2 1875.4 %all-reduce.10.cloned.1.call-start = ((), (), s32[]{:S(2)}) async-start(), calls=%async_computation | async-start | bytes 20037632 | tf_op jit(solution)/shard_map/psum | solution.py:162
  8.5 12.8 copy-start.37
  10.3 11.0 copy-start.42
  22.5 307.9 %copy-start.9 = (bf16[1,288,512]{1,2,0:T(8,128)(2,1)}, bf16[1,288,512]{1,2,0:T(8,128)(2,1)S(1)}, u32[]{:S(2)}) copy-start(bf16[1,288,512]{1,2,0:T(8,128)(2,1)S(1)} %copy.54) | copy-start | bytes 884740
  300.9 29.5 %copy-start.11 = (bf16[1,288,512]{1,2,0:T(8,128)(2,1)S(1)}, bf16[1,288,512]{1,2,0:T(8,128)(2,1)}, u32[]{:S(2)}) copy-start(bf16[1,288,512]{1,2,0:T(8,128)(2,1)} %copy.53) | copy-start | bytes 884740
  334.6 5.3 copy-start.1
  334.6 5.3 copy-start.30
  335.7 338.2 %copy-start.34 = (f32[16,288]{1,0:T(8,128)}, f32[16,288]{1,0:T(8,128)S(1)}, u32[]{:S(2)}) copy-start(f32[16,288]{1,0:T(8,128)S(1)} %fusion.17) | copy-start | bytes 55300
  335.7 6.0 copy-start.8
  335.7 11.4 copy-start.6
  339.8 19.1 %copy-start.48 = (s32[2,12,12]{2,0,1:T(2,128)S(1)}, s32[2,12,12]{2,0,1:T(2,128)}, u32[]{:S(2)}) copy-start(s32[2,12,12]{2,0,1:T(2,128)} %param.23) | copy-start | bytes 3460
  341.6 25.1 %copy-start.45 = (f32[16,1587]{1,0:T(8,128)S(1)}, f32[16,1587]{1,0:T(8,128)}, u32[]{:S(2)}) copy-start(f32[16,1587]{1,0:T(8,128)} %param.21) | copy-start | bytes 304708
  349.3 322.4 %collective-permute-start = (bf16[2,12,6,512]{3,2,1,0:T(8,128)(2,1)}, bf16[2,12,6,512]{3,2,1,0:T(8,128)(2,1)}, u32[]{:S(2)}, u32[]{:S(2)}) collective-permute-start(bf16[2,12,6,512]{3,2,1,0:T(8,128)(2,1)} %get-tuple-element.64), channel_id=1, source_target_pairs={{0,124},{4,0},{8,4},{12,8},{16,12},{20,16},{24,20},{28,24},{32,28}... | collective-permute-start | bytes 442376 | tf_op jit(solution)/shard_map/ppermute | solution.py:15
  641.5 37.5 %copy-start.47 = (f32[512]{0:T(512)S(1)}, f32[512]{0:T(512)}, u32[]{:S(2)}) copy-start(f32[512]{0:T(512)} %param.15) | copy-start | bytes 6148
  672.8 5.2 collective-permute-start.1
  685.5 5.0 copy-start.18
  690.5 2.9 copy-start.2
  690.5 4.0 copy-start.40
  690.5 4.2 copy-start.16
  690.5 4.0 copy-start.24
  694.7 6.2 copy-start.3
  694.7 6.2 copy-start.41
  704.6 494.6 %copy-start.14 = (bf16[16,32,288]{2,1,0:T(8,128)(2,1)}, bf16[16,32,288]{2,1,0:T(8,128)(2,1)S(1)}, u32[]{:S(2)}) copy-start(bf16[16,32,288]{2,1,0:T(8,128)(2,1)S(1)} %convolution_convert_fusion.8) | copy-start | bytes 884740
  705.7 2.9 copy-start.19
  711.2 4.2 copy-start.33
  720.5 6.9 copy-start.21
  720.5 6.9 copy-start.22
  720.5 6.9 copy-start.36
  727.4 470.8 %collective-permute-start.2 = (bf16[2,12,6,512]{3,2,1,0:T(8,128)(2,1)}, bf16[2,12,6,512]{3,2,1,0:T(8,128)(2,1)}, u32[]{:S(2)}, u32[]{:S(2)}) collective-permute-start(bf16[2,12,6,512]{3,2,1,0:T(8,128)(2,1)} %get-tuple-element.59), channel_id=1, source_target_pairs={{0,4},{4,8},{8,12},{12,16},{16,20},{20,24},{24,28},{28,32},{32,36}... | collective-permute-start | bytes 442376 | tf_op jit(solution)/shard_map/ppermute | solution.py:15
  730.1 469.1 %copy-start.25 = (bf16[288,512]{1,0:T(8,128)(2,1)S(1)}, bf16[288,512]{1,0:T(8,128)(2,1)}, u32[]{:S(2)}) copy-start(bf16[288,512]{1,0:T(8,128)(2,1)} %reshape.523) | copy-start | bytes 884740
  730.1 473.5 %copy-start.32 = (bf16[512,512]{1,0:T(8,128)(2,1)S(1)}, bf16[512,512]{1,0:T(8,128)(2,1)}, u32[]{:S(2)}) copy-start(bf16[512,512]{1,0:T(8,128)(2,1)} %param.18) | copy-start | bytes 1572868
  1199.2 2.7 collective-permute-start.3
  1208.4 9.4 slice-start
  1208.4 9.4 copy-start.31
  1208.4 9.4 copy-start.35
  1212.5 5.3 slice-start.1
  1223.1 9.9 copy-start.7
  1223.1 9.9 copy-start.38
  1233.1 7.2 copy-start.23
  1244.0 467.9 %copy-start.13 = (bf16[16,32,288]{2,1,0:T(8,128)(2,1)S(1)}, bf16[16,32,288]{2,1,0:T(8,128)(2,1)}, u32[]{:S(2)}) copy-start(bf16[16,32,288]{2,1,0:T(8,128)(2,1)} %convolution_convert_fusion.9) | copy-start | bytes 884740
  1244.0 468.0 %copy-start.26 = (bf16[288,512]{1,0:T(8,128)(2,1)S(1)}, bf16[288,512]{1,0:T(8,128)(2,1)}, u32[]{:S(2)}) copy-start(bf16[288,512]{1,0:T(8,128)(2,1)} %reshape.522) | copy-start | bytes 884740
  1713.3 6.6 copy-start.17
  1713.3 7.6 copy-start.49
  1713.3 7.6 copy-start.50
  1882.6 9.8 copy-start.28
  1886.8 3.9 copy-start.15
  1886.8 6.6 copy-start.27
  (10 other events, 14.9 us)
Sparse Core Ops, SparseCore 0:
  1713.5 169.0 all-reduce.9
where the time goes:
time: 1910 us; the launch traced here: 1900 us
  other arithmetic  919 us (48%)
  local copies, waits for them, and re-layouts  728 us (38%)
  waiting for transfers between devices  99 us (5%)
  blocking collectives  67.3 us (4%)
  matrix products  62.1 us (3%)
    scatter-add x2, other arithmetic, attend(): bias = table[:, rel_index]  881 us
    gather x4, local copies, waits for them, and re-layouts, attend(): bias = table[:, rel_index]  608 us
    psum x1, waiting for transfers between devices, on_device(): lax.psum((first_grads[0], first_grads[1], first_grads[2], first_grads[3],...  94.3 us
    psum x1, blocking collectives, on_device(): lax.psum((first_grads[0], first_grads[1], first_grads[2], first_grads[3],...  67.3 us
  transfers between devices with their start and end apart: 5, of which 3 were waited for; matrix products, arithmetic and copies ran while one was open for 42% of the time, Pallas kernels for 0%

commit v1 on v0

v1 whole, which is shorter than its diff:
```python
import jax
import jax.numpy as jnp
from jax import lax
from jax.experimental import pallas as pl
from jax.experimental.pallas import tpu as pltpu
from jax.sharding import PartitionSpec as P

F32, BF16, I32 = jnp.float32, jnp.bfloat16, jnp.int32
MESH = pl.DeviceIdType.MESH
D, HEADS, DEPTH, WT, NB = 512, 16, 32, 288, 1587
QUAD, QPAD = 72, 80
PADW, CHUNKS, HIGHS = 384, 13, 7
EPS = 1e-05
LOG2E = 1.4426950408889634
SCALE = DEPTH**-0.5
GROWS, SROWS = 8192, 512
VM = pl.BlockSpec(memory_space=pltpu.VMEM)
SM = pl.BlockSpec(memory_space=pltpu.SMEM)
PARAMS = pltpu.CompilerParams(vmem_limit_bytes=60 << 20)


def quad_row(row_half, col_half, level, row):
    return row_half * 144 + col_half * 72 + level * 36 + row * 6


def dot(a, b):
    return jnp.dot(a, b, preferred_element_type=F32)


def dot_nt(a, b):
    return lax.dot_general(a, b, (((1,), (1,)), ((), ())), preferred_element_type=F32)


def dot_tn(a, b):
    return lax.dot_general(a, b, (((0,), (0,)), ((), ())), preferred_element_type=F32)


def into_quads(src, dst):
    for lev in range(2):
        for r in range(12):
            v = src[lev, r].astype(F32)
            for ch in range(2):
                dst[pl.ds(quad_row(r // 6, ch, lev, r % 6), 6), :] = v[ch * 6 : ch * 6 + 6]


def out_of_quads(src, dst):
    for lev in range(2):
        for r in range(12):
            both = [src[pl.ds(quad_row(r // 6, ch, lev, r % 6), 6), :] for ch in range(2)]
            dst[lev, r] = jnp.concatenate(both, 0).astype(BF16)


def put_quads(value, dst):
    for q in range(4):
        dst[q, :QUAD, :] = value[q * QUAD : (q + 1) * QUAD]
        dst[q, QUAD:, :] = jnp.zeros((QPAD - QUAD, D), dst.dtype)


def get_quads(src):
    return jnp.concatenate([src[q, :QUAD, :].astype(F32) for q in range(4)], 0)


def norm(x):
    xc = x - jnp.mean(x, -1, keepdims=True)
    rstd = lax.rsqrt(jnp.mean(xc * xc, -1, keepdims=True) + EPS)
    return xc * rstd, rstd


def project(h, w_ref, p, pt):
    for n in range(3):
        cols = slice(n * D, n * D + D)
        v = dot(h, w_ref[:, cols])
        p[:, cols] = v.astype(BF16)
        pt[cols, :] = v.T.astype(BF16)


def index_in_quads(rel_ref, rows, highs, lows):
    at = lax.broadcasted_iota(I32, (WT, WT), 0)
    half = (at >= 144).astype(I32)
    rest = at - 144 * half
    col = (rest >= 72).astype(I32)
    rest = rest - 72 * col
    level = (rest >= 36).astype(I32)
    rest = rest - 36 * level
    row = sum((rest >= 6 * k).astype(I32) for k in range(1, 6))
    rest = rest - 6 * row
    natural = level * 144 + (half * 6 + row) * 12 + col * 6 + rest
    perm = (natural == lax.broadcasted_iota(I32, (WT, WT), 1)).astype(F32).astype(BF16)
    rel = rel_ref[...]
    high = (rel >> 8).astype(F32).astype(BF16)
    low = (rel & 255).astype(F32).astype(BF16)

    def moved(part):
        return dot_nt(dot(perm, part).astype(BF16), perm)

    high, low = moved(high), moved(low)
    highs[:, PADW - 128 :] = jnp.zeros((WT, 128), I32)
    lows[:, PADW - 128 :] = jnp.zeros((WT, 128), I32)
    highs[:, :WT] = high.astype(I32)
    lows[:, :WT] = low.astype(I32)


def pack_tables(first_ref, second_ref, packed, step_first, step_second):
    parts = []
    for ref, step_ref in ((first_ref, step_first), (second_ref, step_second)):
        t = ref[...]
        least = jnp.min(t, -1, keepdims=True)
        span = jnp.maximum(jnp.max(t, -1, keepdims=True) - least, 1e-20)
        parts.append(jnp.clip(jnp.floor((t - least) * (65535.0 / span) + 0.5), 0.0, 65535.0).astype(I32))
        step_ref[...] = jnp.broadcast_to(span * (LOG2E / 65535.0), (HEADS, 128))
    packed[:, (CHUNKS - 1) * 128 :] = jnp.zeros((HEADS, 128), I32)
    packed[:, :NB] = (parts[0] << 16) | parts[1]


def gather_bias(packed, highs, lows, bias, start, count):
    @pl.loop(start, start + count)
    def _(r):
        rows = pl.ds(pl.multiple_of(r * 8, 8), 8)
        for ct in range(3):
            lanes = pl.ds(ct * 128, 128)
            high, low = highs[rows, lanes], lows[rows, lanes]
            chunk = high * 2 + (low >> 7)
            lane = low & 127
            masks = [chunk == c for c in range(CHUNKS)]
            for h in range(HEADS):
                acc = None
                for c in range(CHUNKS):
                    row = jnp.broadcast_to(packed[h : h + 1, c * 128 : (c + 1) * 128], (8, 128))
                    found = jnp.take_along_axis(row, lane, axis=1)
                    acc = found if acc is None else jnp.where(masks[c], found, acc)
                bias[h, rows, lanes] = acc


def softmax_head(q, kt, packed, step, high, pen):
    s = dot(q, kt) * (SCALE * LOG2E)
    steps = lax.shift_right_logical(packed, 16) if high else packed & 0xFFFF
    s = s + steps.astype(F32) * step
    if pen is not None:
        s = s + pen
    e = jnp.exp2(s - jnp.max(s, -1, keepdims=True))
    return e * (1.0 / jnp.sum(e, -1, keepdims=True))


def over_heads(p, pt, forward=None, backward=None):
    lanes = lax.broadcasted_iota(I32, (WT, 128), 1) // DEPTH

    @pl.loop(0, 4)
    def _(g):
        g0 = pl.multiple_of(g * 128, 128)
        qg = p[:, pl.ds(g0, 128)]
        kg = p[:, pl.ds(D + g0, 128)]
        vg = p[:, pl.ds(2 * D + g0, 128)]
        ktg = pt[pl.ds(D + g0, 128), :]
        vtg = pt[pl.ds(2 * D + g0, 128), :]
        zero = jnp.zeros_like(qg)
        c_acc = q_acc = None
        if backward is not None:
            dc, dct, a_in, ds_out, dq, dkvt = backward
            dcg = dc[:, pl.ds(g0, 128)]
        for hh in range(4):
            h = g * 4 + hh
            mine = lanes == hh
            if forward is not None:
                bias, steps, high, pen, c, a_out = forward
                a32 = softmax_head(
                    jnp.where(mine, qg, zero),
                    ktg,
                    bias[h, :, :WT],
                    steps[pl.ds(h, 1), 0:1],
                    high,
                    None if pen is None else pen[...],
                )
                a = a32.astype(BF16)
                ch = dot(a, vg)
                c_acc = ch if c_acc is None else jnp.where(mine, ch, c_acc)
                if a_out is not None:
                    a_out[h] = a
            else:
                a = a_in[h]
                a32 = a.astype(F32)
            if backward is not None:
                r0 = pl.multiple_of(g0 + hh * DEPTH, DEPTH)
                da = dot(jnp.where(mine, dcg, zero), vtg)
                ds = a32 * (da - jnp.sum(a32 * da, -1, keepdims=True))
                ds_out[:, h, :WT] = ds
                dsb = ds.astype(BF16)
                dqh = dot(dsb, kg)
                q_acc = dqh if q_acc is None else jnp.where(mine, dqh, q_acc)
                dkvt[pl.ds(r0, DEPTH), :] = (dot(pt[pl.ds(r0, DEPTH), :], dsb) * SCALE).astype(BF16)
                dkvt[pl.ds(D + r0, DEPTH), :] = dot(dct[pl.ds(r0, DEPTH), :], a).astype(BF16)
        if forward is not None:
            c[:, pl.ds(g0, 128)] = c_acc.astype(BF16)
        if backward is not None:
            dq[:, pl.ds(g0, 128)] = (q_acc * SCALE).astype(BF16)


def table_grads(blocks, highs, lows, out):
    out[...] = jnp.zeros_like(out)
    low_of = lax.broadcasted_iota(I32, (256, PADW), 0).astype(F32).astype(BF16)
    one, nil = jnp.ones((256, PADW), BF16), jnp.zeros((256, PADW), BF16)

    @pl.loop(0, WT // 8)
    def _(r):
        rows = pl.ds(pl.multiple_of(r * 8, 8), 8)
        high8 = highs[rows, :].astype(F32).astype(BF16)
        low8 = lows[rows, :].astype(F32).astype(BF16)
        for part in range(2):
            left, right = [], []
            for i in range(part * 4, part * 4 + 4):
                high = jnp.broadcast_to(high8[i : i + 1], (HEADS, PADW))
                low = jnp.broadcast_to(low8[i : i + 1], (256, PADW))
                picked = []
                for block in blocks:
                    ds = block[r * 8 + i].astype(BF16)
                    picked += [jnp.where(high == jnp.array(k, BF16), ds, jnp.zeros_like(ds)) for k in range(HIGHS)]
                left.append(jnp.concatenate(picked, 0))
                right.append(jnp.where(low == low_of, one, nil))
            out[...] += dot_nt(jnp.concatenate(left, 1), jnp.concatenate(right, 1))


def put_columns(value, dst, first):
    for n in range(value.shape[1] // 128):
        at = (first + n) * D
        dst[at : at + D, :] = value[:, n * 128 : (n + 1) * 128].astype(BF16)


def backward_tail(h, xh, rstd, gain, ef, c, e, dq, dkvt, wqkv, grads, g_gain):
    put_columns(dot_tn(h, dq[...]), grads, 0)
    put_columns(dot_nt(h.T, dkvt[...]), grads, 4)
    put_columns(dot_tn(c, e), grads, 12)
    dh = dot_nt(dq[...], wqkv[:, :D]) + dot(wqkv[:, D:], dkvt[...]).T
    dh = dh.astype(BF16).astype(F32)
    g_gain[...] = jnp.sum(dh * xh, 0, keepdims=True)
    dxh = dh * gain
    return rstd * (dxh - jnp.mean(dxh, -1, keepdims=True) - xh * jnp.mean(dxh * xh, -1, keepdims=True)) + ef


def clear_pad(ds):
    ds[:, :, PADW - 128 :] = jnp.zeros((WT, HEADS, 128), F32)


def context_grad(e, wo, dc, dct):
    v = dot_nt(e, wo[...])
    dc[...] = v.astype(BF16)
    dct[...] = v.T.astype(BF16)


def first_forward_kernel(
    tok_ref, gain_ref, wqkv, wo, tab1, tab2, rel_ref,
    y_ref, bias, p, pt, c, a, highs, lows, step1, step2,
    quad, packed,
):
    pack_tables(tab1, tab2, packed, step1, step2)
    index_in_quads(rel_ref, None, highs, lows)
    gather_bias(packed, highs, lows, bias, 0, WT // 8)
    into_quads(tok_ref, quad)
    x = quad[...]
    xh, _ = norm(x)
    project((xh * gain_ref[...]).astype(BF16), wqkv, p, pt)
    over_heads(p, pt, forward=(bias, step1, True, None, c, a))
    put_quads((x + dot(c[...], wo[...])).astype(BF16), y_ref)


def second_kernel(
    z_ref, cot_ref, reg_ref, gain_ref, wqkv, wo, bias, steps,
    mixed_ref, dz_ref, g_gain, grads, ds_out,
    p, pt, c, dc, dct, dq, dkvt, pen, quad,
):
    x = get_quads(z_ref)
    xh, rstd = norm(x)
    h = (xh * gain_ref[...]).astype(BF16)
    project(h, wqkv, p, pt)
    into_quads(cot_ref, quad)
    e = quad[...].astype(BF16)
    context_grad(e, wo, dc, dct)
    split = reg_ref[0, 0, 0] != reg_ref[0, 11, 0]
    lower_row = lax.broadcasted_iota(I32, (WT, WT), 0) >= 144
    lower_col = lax.broadcasted_iota(I32, (WT, WT), 1) >= 144
    pen[...] = jnp.where((lower_row != lower_col) & split, -1e30, 0.0)
    clear_pad(ds_out)
    over_heads(p, pt, (bias, steps, False, pen, c, None), (dc, dct, None, ds_out, dq, dkvt))
    cv = c[...]
    quad[...] = x + dot(cv, wo[...])
    out_of_quads(quad, mixed_ref)
    dz = backward_tail(h, xh, rstd, gain_ref[...], e.astype(F32), cv, e, dq, dkvt, wqkv, grads, g_gain)
    put_quads(dz.astype(BF16), dz_ref)


def first_backward_kernel(
    tok_ref, dy_ref, gain_ref, wqkv, wo, p, pt, c, a, ds2, highs, lows, gain2,
    gt_ref, grads, small,
    dc, dct, dq, dkvt, ds1, quad, sums, g_gain,
):
    into_quads(tok_ref, quad)
    xh, rstd = norm(quad[...])
    h = (xh * gain_ref[...]).astype(BF16)
    ef = get_quads(dy_ref)
    e = ef.astype(BF16)
    context_grad(e, wo, dc, dct)
    clear_pad(ds1)
    over_heads(p, pt, None, (dc, dct, a, ds1, dq, dkvt))
    quad[...] = backward_tail(h, xh, rstd, gain_ref[...], ef, c[...], e, dq, dkvt, wqkv, grads, g_gain)
    out_of_quads(quad, gt_ref)
    table_grads((ds1, ds2), highs, lows, sums)
    small[:224, :] = sums[:, :128].astype(BF16)
    small[224:448, :] = sums[:, 128:].astype(BF16)
    gains = [g[:, n * 128 : (n + 1) * 128] for g in (g_gain, gain2) for n in range(4)]
    gains.append(jnp.zeros((SROWS - 456, 128), F32))
    small[448:, :] = jnp.concatenate(gains, 0).astype(BF16)


def place():
    lon, lat = lax.axis_index("lon"), lax.axis_index("lat")
    x, z, y = lon // 8, (lon // 2) % 4, (lon % 2) * 2 + lat // 2
    return x, y, z, lat % 2


def device(x, y, z, core):
    return {"lon": x * 8 + z * 2 + y // 2, "lat": (y % 2) * 2 + core}


def greet(to):
    barrier = pltpu.get_barrier_semaphore()
    for dev in to:
        pl.semaphore_signal(barrier, inc=1, device_id=dev, device_id_type=MESH)
    pl.semaphore_wait(barrier, len(to))


def shift_kernel(by, src, dst, send, recv, own):
    lon, lat = lax.axis_index("lon"), lax.axis_index("lat")

    def near(step, along_lon, along_lat):
        return {
            "lon": (lon + step * along_lon + 32) % 32,
            "lat": (lat + step * along_lat + 4) % 4,
        }

    moves = [(2, 1, 1, 0), (1, 2, 0, 1), (0, 3, 1, 1)]
    greet([near(-by, m[2], m[3]) for m in moves])
    copies = []
    for n, (here, there, along_lon, along_lat) in enumerate(moves):
        a, b = (here, there) if by < 0 else (there, here)
        copies.append(
            pltpu.make_async_remote_copy(
                src_ref=src.at[a], dst_ref=dst.at[b], send_sem=send.at[n], recv_sem=recv.at[n],
                device_id=near(by, along_lon, along_lat), device_id_type=MESH,
            )
        )
    a, b = (3, 0) if by < 0 else (0, 3)
    for copy in copies:
        copy.start()
    local = pltpu.make_async_copy(src.at[a], dst.at[b], own)
    local.start()
    local.wait()
    for copy in copies:
        copy.wait()


class Job:
    def __init__(self, units, refs, sems, where):
        self.src, self.out, self.r0, self.a, self.r1, self.b, self.r2, self.c4 = refs
        self.send, self.recv = sems
        self.half = self.src.shape[0] // 2
        self.where = where
        self.sets = []
        at = 0
        for n, count in enumerate(units):
            self.sets.append((at, count * 256, (n % 3, (n + 1) % 3, (n + 2) % 3)))
            at += count * 256
        self.live = []

    def peer(self, axis, d):
        to = list(self.where)
        to[axis] = (to[axis] + d) % 4
        return device(*to)

    def copy(self, src, dst, sem, to):
        made = pltpu.make_async_remote_copy(
            src_ref=src, dst_ref=dst, send_sem=self.send.at[sem], recv_sem=self.recv.at[sem],
            device_id=to, device_id_type=MESH,
        )
        made.start()
        self.live.append(made)

    def wait(self):
        for made in self.live:
            made.wait()
        self.live = []

    def other(self):
        x, y, z, core = self.where
        return device(x, y, z, 1 - core)

    def mine(self):
        return pl.multiple_of(self.where[3] * self.half, 128)

    def add(self, dst, dst_at, parts, rows):
        step = 256 if rows % 256 == 0 else rows

        @pl.loop(0, rows // step)
        def _(n):
            total = None
            for ref, lead, at in parts:
                where = pl.ds(pl.multiple_of(at + n * step, 16), step)
                v = (ref[where, :] if lead is None else ref[lead, where, :]).astype(F32)
                total = v if total is None else total + v
            dst[pl.ds(pl.multiple_of(dst_at + n * step, 16), step), :] = total.astype(BF16)

    def stage(self, n):
        if n == 0:
            theirs = pl.multiple_of((1 - self.where[3]) * self.half, 128)
            self.copy(self.src.at[pl.ds(theirs, self.half)], self.r0, 0, self.other())
        if n == 1:
            self.wait()
            self.add(self.a, 0, [(self.src, None, self.mine()), (self.r0, None, 0)], self.half)
            for k, (at, rows, axes) in enumerate(self.sets):
                me = self.where[axes[0]]
                for d in range(1, 4):
                    piece = pl.multiple_of(at + (me + d) % 4 * (rows // 4), 16)
                    self.copy(
                        self.a.at[pl.ds(piece, rows // 4)], self.r1.at[d - 1, pl.ds(at // 4, rows // 4)],
                        1 + k * 3 + d - 1, self.peer(axes[0], d),
                    )
        if n == 2:
            self.wait()
            for k, (at, rows, axes) in enumerate(self.sets):
                own = at + self.where[axes[0]] * (rows // 4)
                self.add(
                    self.b, at // 4, [(self.a, None, own)] + [(self.r1, d, at // 4) for d in range(3)], rows // 4
                )
                me = self.where[axes[1]]
                for d in range(1, 4):
                    piece = pl.multiple_of(at // 4 + (me + d) % 4 * (rows // 16), 16)
                    self.copy(
                        self.b.at[pl.ds(piece, rows // 16)], self.r2.at[d - 1, pl.ds(at // 16, rows // 16)],
                        10 + k * 3 + d - 1, self.peer(axes[1], d),
                    )
        if n == 3:
            self.wait()
            for k, (at, rows, axes) in enumerate(self.sets):
                own = at // 4 + self.where[axes[1]] * (rows // 16)
                me = self.where[axes[2]]
                small = pl.ds(at // 16, rows // 16)
                total = self.b[pl.ds(pl.multiple_of(own, 16), rows // 16), :].astype(F32)
                for d in range(3):
                    total = total + self.r2[d, small, :].astype(F32)
                self.c4[me, small, :] = total.astype(BF16)
                for d in range(1, 4):
                    self.copy(
                        self.c4.at[me, small], self.c4.at[me, small],
                        19 + k * 3 + d - 1, self.peer(axes[2], d),
                    )
        if n == 4:
            self.wait()
            for k, (at, rows, axes) in enumerate(self.sets):
                small = pl.ds(at // 16, rows // 16)
                total = self.c4[0, small, :].astype(F32)
                for d in range(1, 4):
                    total = total + self.c4[d, small, :].astype(F32)
                here = self.mine() + at + self.where[axes[0]] * (rows // 4) + self.where[axes[1]] * (rows // 16)
                spot = pl.ds(pl.multiple_of(here, 16), rows // 16)
                self.out[spot, :] = total.astype(BF16)
                for d in range(1, 4):
                    self.copy(self.out.at[spot], self.out.at[spot], 28 + k * 3 + d - 1, self.peer(axes[1], d))
        if n == 5:
            self.wait()
            for k, (at, rows, axes) in enumerate(self.sets):
                here = self.mine() + at + self.where[axes[0]] * (rows // 4)
                spot = pl.ds(pl.multiple_of(here, 16), rows // 4)
                for d in range(1, 4):
                    self.copy(self.out.at[spot], self.out.at[spot], 37 + k * 3 + d - 1, self.peer(axes[0], d))
        if n == 6:
            self.wait()
            spot = pl.ds(self.mine(), self.half)
            self.copy(self.out.at[spot], self.out.at[spot], 46, self.other())
        if n == 7:
            self.wait()


STAGES = 8
BIG, LITTLE = (6, 5, 5), (1,)


def job_scratch(rows):
    half = rows // 2
    return [
        pltpu.VMEM((half, 128), BF16),
        pltpu.VMEM((half, 128), BF16),
        pltpu.VMEM((3, half // 4, 128), BF16),
        pltpu.VMEM((half // 4, 128), BF16),
        pltpu.VMEM((3, half // 16, 128), BF16),
        pltpu.VMEM((4, half // 16, 128), BF16),
        pltpu.SemaphoreType.DMA((47,)),
        pltpu.SemaphoreType.DMA((47,)),
    ]


def all_peers(where):
    x, y, z, core = where
    to = [device(x, y, z, 1 - core)]
    for axis in range(3):
        for d in range(1, 4):
            at = list(where)
            at[axis] = (at[axis] + d) % 4
            to.append(device(*at))
    return to


def sum_kernel(g2, g1, s, o2, o1, os, *scratch):
    where = place()
    greet(all_peers(where))
    jobs = []
    for n, (units, src, out) in enumerate(((BIG, g2, o2), (BIG, g1, o1), (LITTLE, s, os))):
        mem = scratch[n * 8 : n * 8 + 8]
        jobs.append(Job(units, (src, out) + mem[:6], mem[6:], where))
    for stage in range(STAGES):
        for job in jobs:
            job.stage(stage)


def widen_kernel(s2, s1, small, gq1, gq2, gp1, gp2, gg1, gg2, gt1, gt2):
    for src, gq, gp in ((s1, gq1, gp1), (s2, gq2, gp2)):
        for n in range(12):
            gq[:, n * 128 : (n + 1) * 128] = src[n * D : (n + 1) * D, :].astype(F32)
        for n in range(4):
            gp[:, n * 128 : (n + 1) * 128] = src[(12 + n) * D : (13 + n) * D, :].astype(F32)
    tail = small[448:464, :].astype(F32)
    for b, (gg, gt) in enumerate(((gg1, gt1), (gg2, gt2))):
        for n in range(4):
            gg[:, n * 128 : (n + 1) * 128] = tail[b * 4 + n : b * 4 + n + 1]
        for k in range(2 * HIGHS):
            at = (b * HIGHS + k // 2) * 16 + (k % 2) * 224
            width = min(128, NB - k * 128)
            if width > 0:
                gt[:, k * 128 : k * 128 + width] = small[at : at + 16, :width].astype(F32)


def on_device(
    tokens, cotangent, gain_first, gain_second, qkv_first, qkv_second, proj_first, proj_second,
    table_first, table_second, rel_index, regions,
):
    def arr(shape, dtype=BF16):
        return jax.ShapeDtypeStruct(shape, dtype)

    def mem(*shape, dtype=BF16):
        return pltpu.VMEM(shape, dtype)

    gain_first, gain_second = gain_first.reshape(1, D), gain_second.reshape(1, D)
    grid = arr((2, 12, 12, D))
    quads = arr((4, QPAD, D))
    y, bias, p, pt, c, a, highs, lows, step1, step2 = pl.pallas_call(
        first_forward_kernel,
        out_shape=[
            quads, arr((HEADS, WT, PADW), I32), arr((WT, 3 * D)), arr((3 * D, WT)), arr((WT, D)),
            arr((HEADS, WT, WT)), arr((WT, PADW), I32), arr((WT, PADW), I32),
            arr((HEADS, 128), F32), arr((HEADS, 128), F32),
        ],
        in_specs=[VM] * 7, out_specs=[VM] * 10,
        scratch_shapes=[mem(WT, D, dtype=F32), mem(HEADS, CHUNKS * 128, dtype=I32)],
        compiler_params=PARAMS,
        name="first_forward",
    )(tokens, gain_first, qkv_first, proj_first, table_first, table_second, rel_index)

    def shifted(value, by):
        return pl.pallas_call(
            lambda *refs: shift_kernel(by, *refs),
            out_shape=quads, in_specs=[VM], out_specs=VM,
            scratch_shapes=[pltpu.SemaphoreType.DMA((3,)), pltpu.SemaphoreType.DMA((3,)), pltpu.SemaphoreType.DMA(())],
            compiler_params=pltpu.CompilerParams(collective_id=2 + by, has_side_effects=True),
            name="shift_on" if by < 0 else "shift_back",
        )(value)

    work = [mem(WT, D), mem(D, WT), mem(WT, D), mem(2 * D, WT)]
    mixed, dz, gain2, grads2, ds2 = pl.pallas_call(
        second_kernel,
        out_shape=[grid, quads, arr((1, D), F32), arr((GROWS, 128)), arr((WT, HEADS, PADW), F32)],
        in_specs=[VM, VM, SM] + [VM] * 5, out_specs=[VM] * 5,
        scratch_shapes=[mem(WT, 3 * D), mem(3 * D, WT), mem(WT, D)] + work
        + [mem(WT, WT, dtype=F32), mem(WT, D, dtype=F32)],
        compiler_params=PARAMS,
        name="second_block",
    )(shifted(y, -1), cotangent, regions, gain_second, qkv_second, proj_second, bias, step2)
    grad_tokens, grads1, small = pl.pallas_call(
        first_backward_kernel,
        out_shape=[grid, arr((GROWS, 128)), arr((SROWS, 128))],
        in_specs=[VM] * 13, out_specs=[VM] * 3,
        scratch_shapes=work + [
            mem(WT, HEADS, PADW, dtype=F32), mem(WT, D, dtype=F32), mem(224, 256, dtype=F32), mem(1, D, dtype=F32),
        ],
        compiler_params=PARAMS,
        name="first_backward",
    )(tokens, shifted(dz, 1), gain_first, qkv_first, proj_first, p, pt, c, a, ds2, highs, lows, gain2)
    s2, s1, ss = pl.pallas_call(
        sum_kernel,
        out_shape=[arr((GROWS, 128)), arr((GROWS, 128)), arr((SROWS, 128))],
        in_specs=[VM] * 3, out_specs=[VM] * 3,
        scratch_shapes=job_scratch(GROWS) + job_scratch(GROWS) + job_scratch(SROWS),
        compiler_params=pltpu.CompilerParams(vmem_limit_bytes=60 << 20, collective_id=5, has_side_effects=True),
        name="sum_grads",
    )(grads2, grads1, small)
    gq1, gq2, gp1, gp2, gg1, gg2, gt1, gt2 = pl.pallas_call(
        widen_kernel,
        out_shape=[
            arr((D, 3 * D), F32), arr((D, 3 * D), F32), arr((D, D), F32), arr((D, D), F32),
            arr((1, D), F32), arr((1, D), F32), arr((HEADS, NB), F32), arr((HEADS, NB), F32),
        ],
        in_specs=[VM] * 3, out_specs=[VM] * 8,
        compiler_params=PARAMS,
        name="widen_grads",
    )(s2, s1, ss)
    return mixed, grad_tokens, gg1.reshape(D), gg2.reshape(D), gq1, gq2, gp1, gp2, gt1, gt2


def solution(mesh):
    grid = P(None, "lat", "lon", None)
    return jax.shard_map(
        on_device,
        mesh=mesh,
        in_specs=(grid, grid) + (P(),) * 9 + (P(None, "lat", "lon"),),
        out_specs=(grid, grid) + (P(),) * 8,
        check_vma=False,
    )
```

time: 1910 us -> 200 us (0.10)
  other arithmetic: 919 us -> 0 us
  local copies, waits for them, and re-layouts: 728 us -> 8.87 us
  Pallas kernels: 0 us -> 190 us
  waiting for transfers between devices: 99 us -> 0 us
  blocking collectives: 67.3 us -> 0 us
  matrix products: 62.1 us -> 0 us
    scatter-add x2 -> x0, other arithmetic: 881 us -> none  [attend(): bias = table[:, rel_index]]
    gather x4 -> x0, local copies, waits for them, and re-layouts: 608 us -> none  [attend(): bias = table[:, rel_index]]
    pallas_call x0 -> x7, Pallas kernels: none -> 190 us  [the longest x1 44.9 us: on_device(): pl.pallas_call(sum_kernel, out_shape=[arr((GROWS, 128)), arr((GROWS, 128)...]
    psum x1 -> x0, waiting for transfers between devices: 94.3 us -> none  [on_device(): lax.psum((first_grads[0], first_grads[1], first_grads[2], first_grads[3],...]
    psum x1 -> x0, blocking collectives: 67.3 us -> none  [on_device(): lax.psum((first_grads[0], first_grads[1], first_grads[2], first_grads[3],...]
    dot_general x24 -> x0, matrix products: 62.1 us -> none  [the longest x6 18.7 us: window_attention(): jnp.einsum('hqk,khd->qhd', weights, valueset, preferred_element_type=jnp....]
    select_n x1 -> x0, local copies, waits for them, and re-layouts: 27.7 us -> none  [window_attention(): scores = jnp.where(allowed[None], scores, -1e+30)]
    add_any x1 -> x0, local copies, waits for them, and re-layouts: 27.4 us -> none  [window_attention(): highest = jnp.max(scores, -1, keepdims=True)]
  transfers between devices with their start and end apart: 5 -> 0, of which waited for: 3 -> 0; matrix products, arithmetic and copies ran while one was open for 42% -> 0% of each run, Pallas kernels for 0% -> 0%
where the time goes in v1:
time: 200 us
  Pallas kernels  190 us (95%)
  local copies, waits for them, and re-layouts  8.87 us (4%)
    pallas_call x1, Pallas kernels, on_device(): pl.pallas_call(sum_kernel, out_shape=[arr((GROWS, 128)), arr((GROWS, 128)...  44.9 us
    pallas_call x1, Pallas kernels, on_device(): pl.pallas_call(first_forward_kernel, out_shape=[quads, arr((HEADS, WT, PA...  42.1 us
    pallas_call x1, Pallas kernels, on_device(): pl.pallas_call(first_backward_kernel, out_shape=[grid, arr((GROWS, 128)),...  41.2 us
    pallas_call x2, Pallas kernels, shifted(): pl.pallas_call(lambda *refs: shift_kernel(by, *refs), out_shape=quads, in...  30.6 us
    pallas_call x1, Pallas kernels, on_device(): pl.pallas_call(second_kernel, out_shape=[grid, quads, arr((1, D), F32), a...  25.2 us
    unnamed x5, local copies, waits for them, and re-layouts  8.87 us
    pallas_call x1, Pallas kernels, on_device(): pl.pallas_call(widen_kernel, out_shape=[arr((D, 3 * D), F32), arr((D, 3 *...  5.96 us

profile of v1, /device:TPU:1, one launch (start us, length us, event | category | flops | bytes accessed | tf_op | source)
XLA Modules:
  0.0 199.5 jit_solution(9375488315091963206)
XLA Ops:
  0.6 1.3 copy.24.reg_ref
  2.0 1.8 copy.22.tok_ref
  3.7 1.8 copy.23.cot_ref
  5.5 42.1 %first_forward.1 = (bf16[4,80,512]{2,1,0:T(8,128)(2,1)}, s32[16,288,384]{2,1,0:T(8,128)}, bf16[288,1536]{1,0:T(8,128)(2,1)}, bf16[1536,288]{1,0:T(8,128)(2,1)}, ...) custom-call(bf16[2,12,12,512]{3,2,1,0:T(8,128)(2,1)} %copy.22.tok_re, ...), custom_call_target="tpu_custom_call" | custom-call | tf_op jit(solution)/shard_map/first_forward/pallas_call | solution.py:551
  47.6 15.4 %shift_on.1.z_ref = bf16[4,80,512]{2,1,0:T(8,128)(2,1)} custom-call(bf16[4,80,512]{2,1,0:T(8,128)(2,1)} %get-tuple-element.38.refs_0_), custom_call_target="tpu_custom_call" | custom-call | tf_op jit(solution)/shard_map/shift_on/pallas_call | solution.py:565
  63.0 25.2 %second_block.1 = (bf16[2,12,12,512]{3,2,1,0:T(8,128)(2,1)}, bf16[4,80,512]{2,1,0:T(8,128)(2,1)}, f32[1,512]{1,0:T(1,128)}, bf16[8192,128]{1,0:T(8,128)(2,1)}, f32[288,16,384]{2,1,0:T(8,128)}) custom-call(bf16[4,80,512]{2,1,0:T(8,128)(2,1)} %shift_on.1.z_ref, bf16[2,12,12,512]{3,2,1,0:T(8,128)(2,1)} %copy.23.cot_ref, s32[2,12,12]{2,1,0:T(8,128)} %copy.24.reg_ref, ...), custom_call_target="tpu_custom_call" | custom-call | tf_op jit(solution)/shard_map/second_block/pallas_call | solution.py:574
  88.2 2.0 %copy.26 = bf16[2,12,12,512]{3,0,2,1:T(2,128)(2,1)} copy(bf16[2,12,12,512]{3,2,1,0:T(8,128)(2,1)} %get-tuple-element.66) | data formatting | bytes 589824
  90.2 15.2 %shift_back.1.dy_ref = bf16[4,80,512]{2,1,0:T(8,128)(2,1)} custom-call(bf16[4,80,512]{2,1,0:T(8,128)(2,1)} %get-tuple-element.42.refs_0_), custom_call_target="tpu_custom_call" | custom-call | tf_op jit(solution)/shard_map/shift_back/pallas_call | solution.py:565
  105.4 41.2 %first_backward.1 = (bf16[2,12,12,512]{3,2,1,0:T(8,128)(2,1)}, bf16[8192,128]{1,0:T(8,128)(2,1)}, bf16[512,128]{1,0:T(8,128)(2,1)}) custom-call(bf16[2,12,12,512]{3,2,1,0:T(8,128)(2,1)} %copy.22.tok_ref, bf16[4,80,512]{2,1,0:T(8,128)(2,1)} %shift_back.1.dy_ref, f32[1,512]{1,0:T(1,128)} %bitcast.5, bf16[512,1536]{1,0:T(8,128)(2,1)} %wqkv.5, ...), custom_call_target="tpu_custom_call" | custom-call | tf_op jit(solution)/shard_map/first_backward/pallas_call | solution.py:583
  146.7 2.0 %copy.27 = bf16[2,12,12,512]{3,0,2,1:T(2,128)(2,1)} copy(bf16[2,12,12,512]{3,2,1,0:T(8,128)(2,1)} %get-tuple-element.67) | data formatting | bytes 589824
  148.7 44.9 %sum_grads.1 = (bf16[8192,128]{1,0:T(8,128)(2,1)}, bf16[8192,128]{1,0:T(8,128)(2,1)}, bf16[512,128]{1,0:T(8,128)(2,1)}) custom-call(bf16[8192,128]{1,0:T(8,128)(2,1)} %get-tuple-element.52.g2, bf16[8192,128]{1,0:T(8,128)(2,1)} %get-tuple-element.53.g1, bf16[512,128]{1,0:T(8,128)(2,1)} %get-tuple-element.54.s), custom_call_target="tpu_custom_call" | custom-call | tf_op jit(solution)/shard_map/sum_grads/pallas_call | solution.py:593
  193.5 6.0 %widen_grads.1 = (f32[512,1536]{1,0:T(8,128)}, f32[512,1536]{1,0:T(8,128)}, f32[512,512]{1,0:T(8,128)}, f32[512,512]{1,0:T(8,128)}, f32[1,512]{1,0:T(1,128)}, /*...) custom-call(bf16[8192,128]{1,0:T(8,128)(2,1)} %get-tuple-element.55.s2, ...), custom_call_target="tpu_custom_call" | custom-call | tf_op jit(solution)/shard_map/widen_grads/pallas_call | solution.py:601

commit v2 on v1

--- a/solution.py
+++ b/solution.py
@@ -74,7 +74,7 @@
         pt[cols, :] = v.T.astype(BF16)
 
 
-def index_in_quads(rel_ref, rows, highs, lows):
+def index_in_quads(rel_ref, highs, lows):
     at = lax.broadcasted_iota(I32, (WT, WT), 0)
     half = (at >= 144).astype(I32)
     rest = at - 144 * half
@@ -141,10 +141,10 @@
     return e * (1.0 / jnp.sum(e, -1, keepdims=True))
 
 
-def over_heads(p, pt, forward=None, backward=None):
+def over_heads(p, pt, forward=None, backward=None, groups=(0, 4)):
     lanes = lax.broadcasted_iota(I32, (WT, 128), 1) // DEPTH
 
-    @pl.loop(0, 4)
+    @pl.loop(*groups)
     def _(g):
         g0 = pl.multiple_of(g * 128, 128)
         qg = p[:, pl.ds(g0, 128)]
@@ -194,12 +194,11 @@
             dq[:, pl.ds(g0, 128)] = (q_acc * SCALE).astype(BF16)
 
 
-def table_grads(blocks, highs, lows, out):
-    out[...] = jnp.zeros_like(out)
+def table_grads(blocks, highs, lows, out, start, stop):
     low_of = lax.broadcasted_iota(I32, (256, PADW), 0).astype(F32).astype(BF16)
     one, nil = jnp.ones((256, PADW), BF16), jnp.zeros((256, PADW), BF16)
 
-    @pl.loop(0, WT // 8)
+    @pl.loop(start, stop)
     def _(r):
         rows = pl.ds(pl.multiple_of(r * 8, 8), 8)
         high8 = highs[rows, :].astype(F32).astype(BF16)
@@ -224,10 +223,13 @@
         dst[at : at + D, :] = value[:, n * 128 : (n + 1) * 128].astype(BF16)
 
 
-def backward_tail(h, xh, rstd, gain, ef, c, e, dq, dkvt, wqkv, grads, g_gain):
+def weight_grads(h, c, e, dq, dkvt, grads):
     put_columns(dot_tn(h, dq[...]), grads, 0)
     put_columns(dot_nt(h.T, dkvt[...]), grads, 4)
-    put_columns(dot_tn(c, e), grads, 12)
+    put_columns(dot_tn(c[...], e), grads, 12)
+
+
+def input_grad(xh, rstd, gain, ef, dq, dkvt, wqkv, g_gain):
     dh = dot_nt(dq[...], wqkv[:, :D]) + dot(wqkv[:, D:], dkvt[...]).T
     dh = dh.astype(BF16).astype(F32)
     g_gain[...] = jnp.sum(dh * xh, 0, keepdims=True)
@@ -245,70 +247,6 @@
     dct[...] = v.T.astype(BF16)
 
 
-def first_forward_kernel(
-    tok_ref, gain_ref, wqkv, wo, tab1, tab2, rel_ref,
-    y_ref, bias, p, pt, c, a, highs, lows, step1, step2,
-    quad, packed,
-):
-    pack_tables(tab1, tab2, packed, step1, step2)
-    index_in_quads(rel_ref, None, highs, lows)
-    gather_bias(packed, highs, lows, bias, 0, WT // 8)
-    into_quads(tok_ref, quad)
-    x = quad[...]
-    xh, _ = norm(x)
-    project((xh * gain_ref[...]).astype(BF16), wqkv, p, pt)
-    over_heads(p, pt, forward=(bias, step1, True, None, c, a))
-    put_quads((x + dot(c[...], wo[...])).astype(BF16), y_ref)
-
-
-def second_kernel(
-    z_ref, cot_ref, reg_ref, gain_ref, wqkv, wo, bias, steps,
-    mixed_ref, dz_ref, g_gain, grads, ds_out,
-    p, pt, c, dc, dct, dq, dkvt, pen, quad,
-):
-    x = get_quads(z_ref)
-    xh, rstd = norm(x)
-    h = (xh * gain_ref[...]).astype(BF16)
-    project(h, wqkv, p, pt)
-    into_quads(cot_ref, quad)
-    e = quad[...].astype(BF16)
-    context_grad(e, wo, dc, dct)
-    split = reg_ref[0, 0, 0] != reg_ref[0, 11, 0]
-    lower_row = lax.broadcasted_iota(I32, (WT, WT), 0) >= 144
-    lower_col = lax.broadcasted_iota(I32, (WT, WT), 1) >= 144
-    pen[...] = jnp.where((lower_row != lower_col) & split, -1e30, 0.0)
-    clear_pad(ds_out)
-    over_heads(p, pt, (bias, steps, False, pen, c, None), (dc, dct, None, ds_out, dq, dkvt))
-    cv = c[...]
-    quad[...] = x + dot(cv, wo[...])
-    out_of_quads(quad, mixed_ref)
-    dz = backward_tail(h, xh, rstd, gain_ref[...], e.astype(F32), cv, e, dq, dkvt, wqkv, grads, g_gain)
-    put_quads(dz.astype(BF16), dz_ref)
-
-
-def first_backward_kernel(
-    tok_ref, dy_ref, gain_ref, wqkv, wo, p, pt, c, a, ds2, highs, lows, gain2,
-    gt_ref, grads, small,
-    dc, dct, dq, dkvt, ds1, quad, sums, g_gain,
-):
-    into_quads(tok_ref, quad)
-    xh, rstd = norm(quad[...])
-    h = (xh * gain_ref[...]).astype(BF16)
-    ef = get_quads(dy_ref)
-    e = ef.astype(BF16)
-    context_grad(e, wo, dc, dct)
-    clear_pad(ds1)
-    over_heads(p, pt, None, (dc, dct, a, ds1, dq, dkvt))
-    quad[...] = backward_tail(h, xh, rstd, gain_ref[...], ef, c[...], e, dq, dkvt, wqkv, grads, g_gain)
-    out_of_quads(quad, gt_ref)
-    table_grads((ds1, ds2), highs, lows, sums)
-    small[:224, :] = sums[:, :128].astype(BF16)
-    small[224:448, :] = sums[:, 128:].astype(BF16)
-    gains = [g[:, n * 128 : (n + 1) * 128] for g in (g_gain, gain2) for n in range(4)]
-    gains.append(jnp.zeros((SROWS - 456, 128), F32))
-    small[448:, :] = jnp.concatenate(gains, 0).astype(BF16)
-
-
 def place():
     lon, lat = lax.axis_index("lon"), lax.axis_index("lat")
     x, z, y = lon // 8, (lon // 2) % 4, (lon % 2) * 2 + lat // 2
@@ -319,26 +257,19 @@
     return {"lon": x * 8 + z * 2 + y // 2, "lat": (y % 2) * 2 + core}
 
 
-def greet(to):
-    barrier = pltpu.get_barrier_semaphore()
-    for dev in to:
-        pl.semaphore_signal(barrier, inc=1, device_id=dev, device_id_type=MESH)
-    pl.semaphore_wait(barrier, len(to))
-
-
-def shift_kernel(by, src, dst, send, recv, own):
-    lon, lat = lax.axis_index("lon"), lax.axis_index("lat")
-
-    def near(step, along_lon, along_lat):
-        return {
-            "lon": (lon + step * along_lon + 32) % 32,
-            "lat": (lat + step * along_lat + 4) % 4,
-        }
-
-    moves = [(2, 1, 1, 0), (1, 2, 0, 1), (0, 3, 1, 1)]
-    greet([near(-by, m[2], m[3]) for m in moves])
+def near(step, along_lon, along_lat):
+    return {
+        "lon": (lax.axis_index("lon") + step * along_lon + 32) % 32,
+        "lat": (lax.axis_index("lat") + step * along_lat + 4) % 4,
+    }
+
+
+MOVES = ((2, 1, 1, 0), (1, 2, 0, 1), (0, 3, 1, 1))
+
+
+def shift(by, src, dst, send, recv):
     copies = []
-    for n, (here, there, along_lon, along_lat) in enumerate(moves):
+    for n, (here, there, along_lon, along_lat) in enumerate(MOVES):
         a, b = (here, there) if by < 0 else (there, here)
         copies.append(
             pltpu.make_async_remote_copy(
@@ -346,14 +277,10 @@
                 device_id=near(by, along_lon, along_lat), device_id_type=MESH,
             )
         )
+        copies[-1].start()
     a, b = (3, 0) if by < 0 else (0, 3)
-    for copy in copies:
-        copy.start()
-    local = pltpu.make_async_copy(src.at[a], dst.at[b], own)
-    local.start()
-    local.wait()
-    for copy in copies:
-        copy.wait()
+    dst[b] = src[a]
+    return copies
 
 
 class Job:
@@ -506,16 +433,102 @@
     return to
 
 
-def sum_kernel(g2, g1, s, o2, o1, os, *scratch):
+def kernel(
+    tok_ref, cot_ref, reg_ref, gain1, gain2, wqkv1, wqkv2, wo1, wo2, tab1, tab2, rel_ref,
+    mixed_ref, gt_ref, o2, o1, os,
+    quad, packed, highs, lows, step1, step2, bias, p1, pt1, c1, a1, p2, pt2, c2,
+    dc, dct, dq, dkvt, pen, ds1, ds2, y, z, dz, dy, grads1, grads2, small, g_gain1, g_gain2, sums,
+    send_on, recv_on, send_back, recv_back, *job_mem,
+):
     where = place()
-    greet(all_peers(where))
+    barrier = pltpu.get_barrier_semaphore()
+    peers = all_peers(where) + [near(by, m[2], m[3]) for by in (-1, 1) for m in MOVES]
+    for dev in peers:
+        pl.semaphore_signal(barrier, inc=1, device_id=dev, device_id_type=MESH)
     jobs = []
-    for n, (units, src, out) in enumerate(((BIG, g2, o2), (BIG, g1, o1), (LITTLE, s, os))):
-        mem = scratch[n * 8 : n * 8 + 8]
-        jobs.append(Job(units, (src, out) + mem[:6], mem[6:], where))
-    for stage in range(STAGES):
-        for job in jobs:
-            job.stage(stage)
+    for n, (units, src, out) in enumerate(((BIG, grads2, o2), (BIG, grads1, o1), (LITTLE, small, os))):
+        held = job_mem[n * 8 : n * 8 + 8]
+        jobs.append(Job(units, (src, out) + held[:6], held[6:], where))
+    sum2, sum1, sum_small = (job.stage for job in jobs)
+
+    pack_tables(tab1, tab2, packed, step1, step2)
+    index_in_quads(rel_ref, highs, lows)
+    gather_bias(packed, highs, lows, bias, 0, WT // 8)
+
+    into_quads(tok_ref, quad)
+    x = quad[...]
+    xh, _ = norm(x)
+    project((xh * gain1[...]).astype(BF16), wqkv1, p1, pt1)
+    over_heads(p1, pt1, forward=(bias, step1, True, None, c1, a1))
+    put_quads((x + dot(c1[...], wo1[...])).astype(BF16), y)
+
+    pl.semaphore_wait(barrier, len(peers))
+    on = shift(-1, y, z, send_on, recv_on)
+    into_quads(cot_ref, quad)
+    ef = quad[...]
+    e = ef.astype(BF16)
+    context_grad(e, wo2, dc, dct)
+    split = reg_ref[0, 0, 0] != reg_ref[0, 11, 0]
+    lower_row = lax.broadcasted_iota(I32, (WT, WT), 0) >= 144
+    lower_col = lax.broadcasted_iota(I32, (WT, WT), 1) >= 144
+    pen[...] = jnp.where((lower_row != lower_col) & split, -1e30, 0.0)
+    clear_pad(ds1)
+    clear_pad(ds2)
+    for copy in on:
+        copy.wait()
+
+    x = get_quads(z)
+    xh, rstd = norm(x)
+    h = (xh * gain2[...]).astype(BF16)
+    project(h, wqkv2, p2, pt2)
+    over_heads(p2, pt2, (bias, step2, False, pen, c2, None), (dc, dct, None, ds2, dq, dkvt))
+    put_quads(input_grad(xh, rstd, gain2[...], ef, dq, dkvt, wqkv2, g_gain2).astype(BF16), dz)
+    back = shift(1, dz, dy, send_back, recv_back)
+    weight_grads(h, c2, e, dq, dkvt, grads2)
+    sum2(0)
+    quad[...] = x + dot(c2[...], wo2[...])
+    out_of_quads(quad, mixed_ref)
+
+    into_quads(tok_ref, quad)
+    xh, rstd = norm(quad[...])
+    h = (xh * gain1[...]).astype(BF16)
+    for copy in back:
+        copy.wait()
+    ef = get_quads(dy)
+    e = ef.astype(BF16)
+    context_grad(e, wo1, dc, dct)
+    sum2(1)
+    over_heads(p1, pt1, None, (dc, dct, a1, ds1, dq, dkvt), (0, 2))
+    sum2(2)
+    over_heads(p1, pt1, None, (dc, dct, a1, ds1, dq, dkvt), (2, 4))
+    sum2(3)
+    weight_grads(h, c1, e, dq, dkvt, grads1)
+    sum1(0)
+    sum2(4)
+    quad[...] = input_grad(xh, rstd, gain1[...], ef, dq, dkvt, wqkv1, g_gain1)
+    out_of_quads(quad, gt_ref)
+    sum1(1)
+    sum2(5)
+
+    sums[...] = jnp.zeros_like(sums)
+    for part in range(3):
+        table_grads((ds1, ds2), highs, lows, sums, part * 12, part * 12 + 12)
+        sum1(2 + part)
+        if part < 2:
+            sum2(6 + part)
+    small[:224, :] = sums[:, :128].astype(BF16)
+    small[224:448, :] = sums[:, 128:].astype(BF16)
+    gains = [g[:, n * 128 : (n + 1) * 128] for g in (g_gain1, g_gain2) for n in range(4)]
+    gains.append(jnp.zeros((SROWS - 456, 128), F32))
+    small[448:, :] = jnp.concatenate(gains, 0).astype(BF16)
+    sum_small(0)
+    sum1(5)
+    sum_small(1)
+    sum_small(2)
+    sum1(6)
+    for stage in range(3, 8):
+        sum_small(stage)
+    sum1(7)
 
 
 def widen_kernel(s2, s1, small, gq1, gq2, gp1, gp2, gg1, gg2, gt1, gt2):
@@ -545,59 +558,36 @@
     def mem(*shape, dtype=BF16):
         return pltpu.VMEM(shape, dtype)
 
-    gain_first, gain_second = gain_first.reshape(1, D), gain_second.reshape(1, D)
     grid = arr((2, 12, 12, D))
-    quads = arr((4, QPAD, D))
-    y, bias, p, pt, c, a, highs, lows, step1, step2 = pl.pallas_call(
-        first_forward_kernel,
-        out_shape=[
-            quads, arr((HEADS, WT, PADW), I32), arr((WT, 3 * D)), arr((3 * D, WT)), arr((WT, D)),
-            arr((HEADS, WT, WT)), arr((WT, PADW), I32), arr((WT, PADW), I32),
-            arr((HEADS, 128), F32), arr((HEADS, 128), F32),
-        ],
-        in_specs=[VM] * 7, out_specs=[VM] * 10,
-        scratch_shapes=[mem(WT, D, dtype=F32), mem(HEADS, CHUNKS * 128, dtype=I32)],
-        compiler_params=PARAMS,
-        name="first_forward",
-    )(tokens, gain_first, qkv_first, proj_first, table_first, table_second, rel_index)
-
-    def shifted(value, by):
-        return pl.pallas_call(
-            lambda *refs: shift_kernel(by, *refs),
-            out_shape=quads, in_specs=[VM], out_specs=VM,
-            scratch_shapes=[pltpu.SemaphoreType.DMA((3,)), pltpu.SemaphoreType.DMA((3,)), pltpu.SemaphoreType.DMA(())],
-            compiler_params=pltpu.CompilerParams(collective_id=2 + by, has_side_effects=True),
-            name="shift_on" if by < 0 else "shift_back",
-        )(value)
-
-    work = [mem(WT, D), mem(D, WT), mem(WT, D), mem(2 * D, WT)]
-    mixed, dz, gain2, grads2, ds2 = pl.pallas_call(
-        second_kernel,
-        out_shape=[grid, quads, arr((1, D), F32), arr((GROWS, 128)), arr((WT, HEADS, PADW), F32)],
-        in_specs=[VM, VM, SM] + [VM] * 5, out_specs=[VM] * 5,
-        scratch_shapes=[mem(WT, 3 * D), mem(3 * D, WT), mem(WT, D)] + work
-        + [mem(WT, WT, dtype=F32), mem(WT, D, dtype=F32)],
-        compiler_params=PARAMS,
-        name="second_block",
-    )(shifted(y, -1), cotangent, regions, gain_second, qkv_second, proj_second, bias, step2)
-    grad_tokens, grads1, small = pl.pallas_call(
-        first_backward_kernel,
-        out_shape=[grid, arr((GROWS, 128)), arr((SROWS, 128))],
-        in_specs=[VM] * 13, out_specs=[VM] * 3,
-        scratch_shapes=work + [
-            mem(WT, HEADS, PADW, dtype=F32), mem(WT, D, dtype=F32), mem(224, 256, dtype=F32), mem(1, D, dtype=F32),
-        ],
-        compiler_params=PARAMS,
-        name="first_backward",
-    )(tokens, shifted(dz, 1), gain_first, qkv_first, proj_first, p, pt, c, a, ds2, highs, lows, gain2)
-    s2, s1, ss = pl.pallas_call(
-        sum_kernel,
-        out_shape=[arr((GROWS, 128)), arr((GROWS, 128)), arr((SROWS, 128))],
-        in_specs=[VM] * 3, out_specs=[VM] * 3,
-        scratch_shapes=job_scratch(GROWS) + job_scratch(GROWS) + job_scratch(SROWS),
-        compiler_params=pltpu.CompilerParams(vmem_limit_bytes=60 << 20, collective_id=5, has_side_effects=True),
-        name="sum_grads",
-    )(grads2, grads1, small)
+    big, little = arr((GROWS, 128)), arr((SROWS, 128))
+    three = pltpu.SemaphoreType.DMA((3,))
+    mixed, grad_tokens, s2, s1, ss = pl.pallas_call(
+        kernel,
+        out_shape=[grid, grid, big, big, little],
+        in_specs=[VM, VM, SM] + [VM] * 9,
+        out_specs=[VM] * 5,
+        scratch_shapes=[
+            mem(WT, D, dtype=F32), mem(HEADS, CHUNKS * 128, dtype=I32),
+            mem(WT, PADW, dtype=I32), mem(WT, PADW, dtype=I32), mem(HEADS, 128, dtype=F32), mem(HEADS, 128, dtype=F32),
+            mem(HEADS, WT, PADW, dtype=I32),
+            mem(WT, 3 * D), mem(3 * D, WT), mem(WT, D), mem(HEADS, WT, WT),
+            mem(WT, 3 * D), mem(3 * D, WT), mem(WT, D),
+            mem(WT, D), mem(D, WT), mem(WT, D), mem(2 * D, WT), mem(WT, WT, dtype=F32),
+            mem(WT, HEADS, PADW, dtype=F32), mem(WT, HEADS, PADW, dtype=F32),
+        ]
+        + [mem(4, QPAD, D)] * 4
+        + [
+            mem(GROWS, 128), mem(GROWS, 128), mem(SROWS, 128),
+            mem(1, D, dtype=F32), mem(1, D, dtype=F32), mem(224, 256, dtype=F32),
+            three, three, three, three,
+        ]
+        + job_scratch(GROWS) + job_scratch(GROWS) + job_scratch(SROWS),
+        compiler_params=pltpu.CompilerParams(vmem_limit_bytes=62 << 20, collective_id=3, has_side_effects=True),
+        name="window_pair",
+    )(
+        tokens, cotangent, regions, gain_first.reshape(1, D), gain_second.reshape(1, D), qkv_first, qkv_second,
+        proj_first, proj_second, table_first, table_second, rel_index,
+    )
     gq1, gq2, gp1, gp2, gg1, gg2, gt1, gt2 = pl.pallas_call(
         widen_kernel,
         out_shape=[

time: 200 us -> 165 us (0.82)
  Pallas kernels: 190 us -> 155 us
    pallas_call x6 -> x1, Pallas kernels: 184 us -> 149 us  [on_device(): pl.pallas_call(kernel, out_shape=[grid, grid, big, big, little], in_specs...]
where the time goes in v2:
time: 165 us; the launch traced here: 164 us
  Pallas kernels  155 us (94%)
  local copies, waits for them, and re-layouts  8.87 us (5%)
    pallas_call x1, Pallas kernels, on_device(): pl.pallas_call(kernel, out_shape=[grid, grid, big, big, little], in_specs...  149 us
    unnamed x5, local copies, waits for them, and re-layouts  8.87 us
    pallas_call x1, Pallas kernels, on_device(): pl.pallas_call(widen_kernel, out_shape=[arr((D, 3 * D), F32), arr((D, 3 *...  5.95 us

profile of v2, /device:TPU:1, one launch (start us, length us, event | category | flops | bytes accessed | tf_op | source)
XLA Modules:
  0.0 164.4 jit_solution(1158461413335281946)
XLA Ops:
  0.6 1.3 copy.24.reg_ref
  2.0 1.8 %copy.22.tok_ref = bf16[2,12,12,512]{3,2,1,0:T(8,128)(2,1)} copy(bf16[2,12,12,512]{3,0,2,1:T(2,128)(2,1)} %param.12) | data formatting | bytes 589824 | tf_op args[0]
  3.7 1.8 %copy.23.cot_ref = bf16[2,12,12,512]{3,2,1,0:T(8,128)(2,1)} copy(bf16[2,12,12,512]{3,0,2,1:T(2,128)(2,1)} %param.13) | data formatting | bytes 589824 | tf_op args[1]
  5.5 149.0 %window_pair.1 = (bf16[2,12,12,512]{3,2,1,0:T(8,128)(2,1)}, bf16[2,12,12,512]{3,2,1,0:T(8,128)(2,1)}, bf16[8192,128]{1,0:T(8,128)(2,1)}, bf16[8192,128]{1,0:T(8,128)(2,1)}, bf16[512,128]{1,0:T(8,128)(2,1)}) custom-call(bf16[2,12,12,512]{3,2,1,0:T(8,128)(2,1)} %copy.22.tok_ref, bf16[2,12,12,512]{3,2,1,0:T(8,128)(2,1)} %copy.23.cot_ref, ...), custom_call_target="tpu_custom_call" | custom-call | tf_op jit(solution)/shard_map/window_pair/pallas_call | solution.py:564
  154.5 2.0 %copy.25 = bf16[2,12,12,512]{3,0,2,1:T(2,128)(2,1)} copy(bf16[2,12,12,512]{3,2,1,0:T(8,128)(2,1)} %get-tuple-element.36) | data formatting | bytes 589824
  156.5 2.0 %copy.26 = bf16[2,12,12,512]{3,0,2,1:T(2,128)(2,1)} copy(bf16[2,12,12,512]{3,2,1,0:T(8,128)(2,1)} %get-tuple-element.37) | data formatting | bytes 589824
  158.5 6.0 %widen_grads.1 = (f32[512,1536]{1,0:T(8,128)}, f32[512,1536]{1,0:T(8,128)}, f32[512,512]{1,0:T(8,128)}, f32[512,512]{1,0:T(8,128)}, f32[1,512]{1,0:T(1,128)}, /*...) custom-call(bf16[8192,128]{1,0:T(8,128)(2,1)} %get-tuple-element.25.s2, ...), custom_call_target="tpu_custom_call" | custom-call | tf_op jit(solution)/shard_map/widen_grads/pallas_call | solution.py:591

commit v3 on v2

--- a/solution.py
+++ b/solution.py
@@ -19,8 +19,8 @@
 PARAMS = pltpu.CompilerParams(vmem_limit_bytes=60 << 20)
 
 
-def quad_row(row_half, col_half, level, row):
-    return row_half * 144 + col_half * 72 + level * 36 + row * 6
+def quad_row(row, col_half):
+    return row // 6 * 144 + col_half * 72 + row % 6 * 12
 
 
 def dot(a, b):
@@ -36,18 +36,16 @@
 
 
 def into_quads(src, dst):
-    for lev in range(2):
-        for r in range(12):
-            v = src[lev, r].astype(F32)
-            for ch in range(2):
-                dst[pl.ds(quad_row(r // 6, ch, lev, r % 6), 6), :] = v[ch * 6 : ch * 6 + 6]
+    for r in range(12):
+        v = src[r].astype(F32).reshape(24, D)
+        for ch in range(2):
+            dst[pl.ds(quad_row(r, ch), 12), :] = v[ch * 12 : ch * 12 + 12]
 
 
 def out_of_quads(src, dst):
-    for lev in range(2):
-        for r in range(12):
-            both = [src[pl.ds(quad_row(r // 6, ch, lev, r % 6), 6), :] for ch in range(2)]
-            dst[lev, r] = jnp.concatenate(both, 0).astype(BF16)
+    for r in range(12):
+        both = [src[pl.ds(quad_row(r, ch), 12), :] for ch in range(2)]
+        dst[r] = jnp.concatenate(both, 0).reshape(12, 2, D).astype(BF16)
 
 
 def put_quads(value, dst):
@@ -80,11 +78,9 @@
     rest = at - 144 * half
     col = (rest >= 72).astype(I32)
     rest = rest - 72 * col
-    level = (rest >= 36).astype(I32)
-    rest = rest - 36 * level
-    row = sum((rest >= 6 * k).astype(I32) for k in range(1, 6))
-    rest = rest - 6 * row
-    natural = level * 144 + (half * 6 + row) * 12 + col * 6 + rest
+    row = sum((rest >= 12 * k).astype(I32) for k in range(1, 6))
+    rest = rest - 12 * row
+    natural = (rest & 1) * 144 + (half * 6 + row) * 12 + col * 6 + (rest >> 1)
     perm = (natural == lax.broadcasted_iota(I32, (WT, WT), 1)).astype(F32).astype(BF16)
     rel = rel_ref[...]
     high = (rel >> 8).astype(F32).astype(BF16)
@@ -194,11 +190,11 @@
             dq[:, pl.ds(g0, 128)] = (q_acc * SCALE).astype(BF16)
 
 
-def table_grads(blocks, highs, lows, out, start, stop):
+def table_grads(blocks, highs, lows, out, first, start, stop):
     low_of = lax.broadcasted_iota(I32, (256, PADW), 0).astype(F32).astype(BF16)
     one, nil = jnp.ones((256, PADW), BF16), jnp.zeros((256, PADW), BF16)
 
-    @pl.loop(start, stop)
+    @pl.loop(first + start, first + stop)
     def _(r):
         rows = pl.ds(pl.multiple_of(r * 8, 8), 8)
         high8 = highs[rows, :].astype(F32).astype(BF16)
@@ -209,8 +205,8 @@
                 high = jnp.broadcast_to(high8[i : i + 1], (HEADS, PADW))
                 low = jnp.broadcast_to(low8[i : i + 1], (256, PADW))
                 picked = []
-                for block in blocks:
-                    ds = block[r * 8 + i].astype(BF16)
+                for block, theirs in blocks:
+                    ds = (block[r * 8 + i] + theirs[(r - first) * 8 + i]).astype(BF16)
                     picked += [jnp.where(high == jnp.array(k, BF16), ds, jnp.zeros_like(ds)) for k in range(HIGHS)]
                 left.append(jnp.concatenate(picked, 0))
                 right.append(jnp.where(low == low_of, one, nil))
@@ -223,10 +219,9 @@
         dst[at : at + D, :] = value[:, n * 128 : (n + 1) * 128].astype(BF16)
 
 
-def weight_grads(h, c, e, dq, dkvt, grads):
+def qkv_grads(h, dq, dkvt, grads):
     put_columns(dot_tn(h, dq[...]), grads, 0)
     put_columns(dot_nt(h.T, dkvt[...]), grads, 4)
-    put_columns(dot_tn(c[...], e), grads, 12)
 
 
 def input_grad(xh, rstd, gain, ef, dq, dkvt, wqkv, g_gain):
@@ -404,8 +399,69 @@
             self.wait()
 
 
-STAGES = 8
-BIG, LITTLE = (6, 5, 5), (1,)
+class SmallJob(Job):
+    def __init__(self, refs, sems, where):
+        self.src, self.out, self.r0, self.a, self.r1, self.c4 = refs
+        self.send, self.recv = sems
+        self.half = self.src.shape[0] // 2
+        self.where = where
+        self.live = []
+
+    def plane(self):
+        x, y, z, core = self.where
+        me = x * 4 + z
+        for d in range(1, 16):
+            to = (me + d) % 16
+            yield d, me, to, device(to // 4, y, to % 4, core)
+
+    def stage(self, n):
+        x, y, z, core = self.where
+        me = x * 4 + z
+        if n == 0:
+            Job.stage(self, 0)
+        if n == 1:
+            self.wait()
+            total = self.src[pl.ds(self.mine(), self.half), :].astype(F32) + self.r0[...].astype(F32)
+            self.a[...] = total.astype(BF16)
+            self.r1[me] = self.a[pl.ds(pl.multiple_of(me * 16, 16), 16), :]
+            for d, me, to, dev in self.plane():
+                self.copy(self.a.at[pl.ds(pl.multiple_of(to * 16, 16), 16)], self.r1.at[me], d, dev)
+        if n == 2:
+            self.wait()
+            total = self.r1[0].astype(F32)
+            for k in range(1, 16):
+                total = total + self.r1[k].astype(F32)
+            self.c4[y] = total.astype(BF16)
+            for d in range(1, 4):
+                self.copy(self.c4.at[y], self.c4.at[y], 15 + d, device(x, (y + d) % 4, z, core))
+        if n == 3:
+            self.wait()
+            total = self.c4[0].astype(F32)
+            for k in range(1, 4):
+                total = total + self.c4[k].astype(F32)
+            spot = pl.ds(pl.multiple_of(self.mine() + me * 16, 16), 16)
+            self.out[spot, :] = total.astype(BF16)
+            for d, me, to, dev in self.plane():
+                self.copy(self.out.at[spot], self.out.at[spot], 18 + d, dev)
+        if n == 4:
+            Job.stage(self, 6)
+        if n == 5:
+            self.wait()
+
+
+UNITS = {8192: (6, 5, 5), 6144: (4, 4, 4), 2048: (2, 1, 1)}
+
+
+def small_scratch():
+    half = SROWS // 2
+    return [
+        pltpu.VMEM((half, 128), BF16),
+        pltpu.VMEM((half, 128), BF16),
+        pltpu.VMEM((16, 16, 128), BF16),
+        pltpu.VMEM((4, 16, 128), BF16),
+        pltpu.SemaphoreType.DMA((47,)),
+        pltpu.SemaphoreType.DMA((47,)),
+    ]
 
 
 def job_scratch(rows):
@@ -430,50 +486,76 @@
             at = list(where)
             at[axis] = (at[axis] + d) % 4
             to.append(device(*at))
+    for dx in range(1, 4):
+        for dz in range(1, 4):
+            to.append(device((x + dx) % 4, y, (z + dz) % 4, core))
     return to
 
 
 def kernel(
     tok_ref, cot_ref, reg_ref, gain1, gain2, wqkv1, wqkv2, wo1, wo2, tab1, tab2, rel_ref,
-    mixed_ref, gt_ref, o2, o1, os,
+    mixed_ref, gt_ref, o2, oq, oo, os,
     quad, packed, highs, lows, step1, step2, bias, p1, pt1, c1, a1, p2, pt2, c2,
-    dc, dct, dq, dkvt, pen, ds1, ds2, y, z, dz, dy, grads1, grads2, small, g_gain1, g_gain2, sums,
-    send_on, recv_on, send_back, recv_back, *job_mem,
+    dc, dct, dq, dkvt, pen, ds1, ds2, their_ds1, their_ds2, y, z, dz, dy,
+    small, g_gain1, g_gain2, sums,
+    send_on, recv_on, send_back, recv_back, pair_send, pair_recv, *job_mem,
 ):
     where = place()
+    core = where[3]
     barrier = pltpu.get_barrier_semaphore()
     peers = all_peers(where) + [near(by, m[2], m[3]) for by in (-1, 1) for m in MOVES]
     for dev in peers:
         pl.semaphore_signal(barrier, inc=1, device_id=dev, device_id_type=MESH)
     jobs = []
-    for n, (units, src, out) in enumerate(((BIG, grads2, o2), (BIG, grads1, o1), (LITTLE, small, os))):
+    for n, ref in enumerate((o2, oq, oo)):
         held = job_mem[n * 8 : n * 8 + 8]
-        jobs.append(Job(units, (src, out) + held[:6], held[6:], where))
-    sum2, sum1, sum_small = (job.stage for job in jobs)
+        jobs.append(Job(UNITS[ref.shape[0]], (ref, ref) + held[:6], held[6:], where))
+    sum2, sum_q, sum_o = (job.stage for job in jobs)
+    held = job_mem[24:]
+    sum_s = SmallJob((small, os) + held[:4], held[4:], where).stage
+
+    def to_pair(n, src, dst):
+        copy = pltpu.make_async_remote_copy(
+            src_ref=src, dst_ref=dst, send_sem=pair_send.at[n], recv_sem=pair_recv.at[n],
+            device_id=device(*where[:3], 1 - core), device_id_type=MESH,
+        )
+        copy.start()
+        return copy
+
+    mine = pl.multiple_of(core * 144, 16)
+    theirs = pl.multiple_of((1 - core) * 144, 16)
+    first = core * 18
 
     pack_tables(tab1, tab2, packed, step1, step2)
     index_in_quads(rel_ref, highs, lows)
-    gather_bias(packed, highs, lows, bias, 0, WT // 8)
+    pl.semaphore_wait(barrier, len(peers))
+    sent = []
+    for part in range(3):
+        gather_bias(packed, highs, lows, bias, first + part * 6, 6)
+        rows = pl.ds(pl.multiple_of(mine + part * 48, 16), 48)
+        sent.append(to_pair(part, bias.at[:, rows], bias.at[:, rows]))
 
     into_quads(tok_ref, quad)
     x = quad[...]
     xh, _ = norm(x)
     project((xh * gain1[...]).astype(BF16), wqkv1, p1, pt1)
+    for copy in sent:
+        copy.wait()
     over_heads(p1, pt1, forward=(bias, step1, True, None, c1, a1))
     put_quads((x + dot(c1[...], wo1[...])).astype(BF16), y)
 
-    pl.semaphore_wait(barrier, len(peers))
     on = shift(-1, y, z, send_on, recv_on)
     into_quads(cot_ref, quad)
     ef = quad[...]
     e = ef.astype(BF16)
     context_grad(e, wo2, dc, dct)
-    split = reg_ref[0, 0, 0] != reg_ref[0, 11, 0]
+    split = reg_ref[0, 0, 0] != reg_ref[11, 0, 0]
     lower_row = lax.broadcasted_iota(I32, (WT, WT), 0) >= 144
     lower_col = lax.broadcasted_iota(I32, (WT, WT), 1) >= 144
     pen[...] = jnp.where((lower_row != lower_col) & split, -1e30, 0.0)
     clear_pad(ds1)
     clear_pad(ds2)
+    sums[...] = jnp.zeros_like(sums)
     for copy in on:
         copy.wait()
 
@@ -484,7 +566,9 @@
     over_heads(p2, pt2, (bias, step2, False, pen, c2, None), (dc, dct, None, ds2, dq, dkvt))
     put_quads(input_grad(xh, rstd, gain2[...], ef, dq, dkvt, wqkv2, g_gain2).astype(BF16), dz)
     back = shift(1, dz, dy, send_back, recv_back)
-    weight_grads(h, c2, e, dq, dkvt, grads2)
+    ds_sent = [to_pair(3, ds2.at[pl.ds(theirs, 144)], their_ds2)]
+    qkv_grads(h, dq, dkvt, o2)
+    put_columns(dot_tn(c2[...], e), o2, 12)
     sum2(0)
     quad[...] = x + dot(c2[...], wo2[...])
     out_of_quads(quad, mixed_ref)
@@ -496,55 +580,67 @@
         copy.wait()
     ef = get_quads(dy)
     e = ef.astype(BF16)
+    put_columns(dot_tn(c1[...], e), oo, 0)
+    sum2(1)
+    sum_o(0)
     context_grad(e, wo1, dc, dct)
-    sum2(1)
+    sum_o(1)
     over_heads(p1, pt1, None, (dc, dct, a1, ds1, dq, dkvt), (0, 2))
     sum2(2)
+    sum_o(2)
     over_heads(p1, pt1, None, (dc, dct, a1, ds1, dq, dkvt), (2, 4))
+    ds_sent.append(to_pair(4, ds1.at[pl.ds(theirs, 144)], their_ds1))
     sum2(3)
-    weight_grads(h, c1, e, dq, dkvt, grads1)
-    sum1(0)
+    sum_o(3)
+    qkv_grads(h, dq, dkvt, oq)
+    sum_q(0)
     sum2(4)
+    sum_o(4)
     quad[...] = input_grad(xh, rstd, gain1[...], ef, dq, dkvt, wqkv1, g_gain1)
+    sum_q(1)
+    sum2(5)
     out_of_quads(quad, gt_ref)
-    sum1(1)
-    sum2(5)
-
-    sums[...] = jnp.zeros_like(sums)
+    sum_o(5)
+    for copy in ds_sent:
+        copy.wait()
+
+    blocks = ((ds1, their_ds1), (ds2, their_ds2))
     for part in range(3):
-        table_grads((ds1, ds2), highs, lows, sums, part * 12, part * 12 + 12)
-        sum1(2 + part)
-        if part < 2:
-            sum2(6 + part)
+        table_grads(blocks, highs, lows, sums, first, part * 6, part * 6 + 6)
+        sum_q(2 + part)
+        if part > 0:
+            sum2(5 + part)
+            sum_o(5 + part)
     small[:224, :] = sums[:, :128].astype(BF16)
     small[224:448, :] = sums[:, 128:].astype(BF16)
     gains = [g[:, n * 128 : (n + 1) * 128] for g in (g_gain1, g_gain2) for n in range(4)]
     gains.append(jnp.zeros((SROWS - 456, 128), F32))
     small[448:, :] = jnp.concatenate(gains, 0).astype(BF16)
-    sum_small(0)
-    sum1(5)
-    sum_small(1)
-    sum_small(2)
-    sum1(6)
-    for stage in range(3, 8):
-        sum_small(stage)
-    sum1(7)
-
-
-def widen_kernel(s2, s1, small, gq1, gq2, gp1, gp2, gg1, gg2, gt1, gt2):
-    for src, gq, gp in ((s1, gq1, gp1), (s2, gq2, gp2)):
-        for n in range(12):
-            gq[:, n * 128 : (n + 1) * 128] = src[n * D : (n + 1) * D, :].astype(F32)
-        for n in range(4):
-            gp[:, n * 128 : (n + 1) * 128] = src[(12 + n) * D : (13 + n) * D, :].astype(F32)
-    tail = small[448:464, :].astype(F32)
-    for b, (gg, gt) in enumerate(((gg1, gt1), (gg2, gt2))):
-        for n in range(4):
-            gg[:, n * 128 : (n + 1) * 128] = tail[b * 4 + n : b * 4 + n + 1]
-        for k in range(2 * HIGHS):
-            at = (b * HIGHS + k // 2) * 16 + (k % 2) * 224
-            width = min(128, NB - k * 128)
-            if width > 0:
+    sum_s(0)
+    sum_s(1)
+    sum_q(5)
+    sum_s(2)
+    sum_s(3)
+    sum_q(6)
+    sum_s(4)
+    sum_s(5)
+    sum_q(7)
+
+
+def widen_kernel(s2, sq, so, small, gq1, gq2, gp1, gp2, gg1, gg2, gt1, gt2):
+    for src, at, dst in ((sq, 0, gq1), (so, 0, gp1), (s2, 0, gq2), (s2, 12, gp2)):
+        for n in range(dst.shape[1] // 128):
+            dst[:, n * 128 : (n + 1) * 128] = src[at + n].astype(F32)
+
+    @pl.when(pl.program_id(0) == 0)
+    def _():
+        tail = small[448:464, :].astype(F32)
+        for b, (gg, gt) in enumerate(((gg1, gt1), (gg2, gt2))):
+            for n in range(4):
+                gg[:, n * 128 : (n + 1) * 128] = tail[b * 4 + n : b * 4 + n + 1]
+            for k in range(CHUNKS):
+                at = (b * HIGHS + k // 2) * 16 + (k % 2) * 224
+                width = min(128, NB - k * 128)
                 gt[:, k * 128 : k * 128 + width] = small[at : at + 16, :width].astype(F32)
 
 
@@ -558,14 +654,15 @@
     def mem(*shape, dtype=BF16):
         return pltpu.VMEM(shape, dtype)
 
-    grid = arr((2, 12, 12, D))
-    big, little = arr((GROWS, 128)), arr((SROWS, 128))
+    grid = arr((12, 12, 2, D))
+    rows = (8192, 6144, 2048)
     three = pltpu.SemaphoreType.DMA((3,))
-    mixed, grad_tokens, s2, s1, ss = pl.pallas_call(
+    five = pltpu.SemaphoreType.DMA((5,))
+    mixed, grad_tokens, s2, sq, so, small = pl.pallas_call(
         kernel,
-        out_shape=[grid, grid, big, big, little],
+        out_shape=[grid, grid] + [arr((n, 128)) for n in rows] + [arr((SROWS, 128))],
         in_specs=[VM, VM, SM] + [VM] * 9,
-        out_specs=[VM] * 5,
+        out_specs=[VM] * 6,
         scratch_shapes=[
             mem(WT, D, dtype=F32), mem(HEADS, CHUNKS * 128, dtype=I32),
             mem(WT, PADW, dtype=I32), mem(WT, PADW, dtype=I32), mem(HEADS, 128, dtype=F32), mem(HEADS, 128, dtype=F32),
@@ -574,30 +671,42 @@
             mem(WT, 3 * D), mem(3 * D, WT), mem(WT, D),
             mem(WT, D), mem(D, WT), mem(WT, D), mem(2 * D, WT), mem(WT, WT, dtype=F32),
             mem(WT, HEADS, PADW, dtype=F32), mem(WT, HEADS, PADW, dtype=F32),
+            mem(144, HEADS, PADW, dtype=F32), mem(144, HEADS, PADW, dtype=F32),
         ]
         + [mem(4, QPAD, D)] * 4
-        + [
-            mem(GROWS, 128), mem(GROWS, 128), mem(SROWS, 128),
-            mem(1, D, dtype=F32), mem(1, D, dtype=F32), mem(224, 256, dtype=F32),
-            three, three, three, three,
-        ]
-        + job_scratch(GROWS) + job_scratch(GROWS) + job_scratch(SROWS),
+        + [mem(SROWS, 128), mem(1, D, dtype=F32), mem(1, D, dtype=F32), mem(224, 256, dtype=F32)]
+        + [three] * 4 + [five] * 2
+        + [ref for n in rows for ref in job_scratch(n)] + small_scratch(),
         compiler_params=pltpu.CompilerParams(vmem_limit_bytes=62 << 20, collective_id=3, has_side_effects=True),
         name="window_pair",
     )(
-        tokens, cotangent, regions, gain_first.reshape(1, D), gain_second.reshape(1, D), qkv_first, qkv_second,
+        tokens.transpose(1, 2, 0, 3), cotangent.transpose(1, 2, 0, 3), regions.transpose(1, 0, 2),
+        gain_first.reshape(1, D), gain_second.reshape(1, D), qkv_first, qkv_second,
         proj_first, proj_second, table_first, table_second, rel_index,
     )
+
+    def part(*shape):
+        return pl.BlockSpec(shape, lambda i: (0, i, 0) if len(shape) == 3 else (i, 0))
+
+    def whole(*shape):
+        return pl.BlockSpec(shape, lambda i: (0, 0))
+
     gq1, gq2, gp1, gp2, gg1, gg2, gt1, gt2 = pl.pallas_call(
         widen_kernel,
         out_shape=[
             arr((D, 3 * D), F32), arr((D, 3 * D), F32), arr((D, D), F32), arr((D, D), F32),
             arr((1, D), F32), arr((1, D), F32), arr((HEADS, NB), F32), arr((HEADS, NB), F32),
         ],
-        in_specs=[VM] * 3, out_specs=[VM] * 8,
+        grid=(4,),
+        in_specs=[part(16, 128, 128), part(12, 128, 128), part(4, 128, 128), whole(SROWS, 128)],
+        out_specs=[
+            part(128, 3 * D), part(128, 3 * D), part(128, D), part(128, D),
+            whole(1, D), whole(1, D), whole(HEADS, NB), whole(HEADS, NB),
+        ],
         compiler_params=PARAMS,
         name="widen_grads",
-    )(s2, s1, ss)
+    )(s2.reshape(16, D, 128), sq.reshape(12, D, 128), so.reshape(4, D, 128), small)
+    mixed, grad_tokens = mixed.transpose(2, 0, 1, 3), grad_tokens.transpose(2, 0, 1, 3)
     return mixed, grad_tokens, gg1.reshape(D), gg2.reshape(D), gq1, gq2, gp1, gp2, gt1, gt2
 
 

time: 165 us -> 136 us (0.82)
  Pallas kernels: 155 us -> 134 us
  local copies, waits for them, and re-layouts: 8.87 us -> 1.44 us
    pallas_call x1, Pallas kernels: 149 us -> 127 us  [on_device(): pl.pallas_call(kernel, out_shape=[grid, grid] + [arr((n, 128)) for n in r...]
    unnamed x5 -> x6, local copies, waits for them, and re-layouts: 8.87 us -> 1.44 us
where the time goes in v3:
time: 136 us
  Pallas kernels  134 us (99%)
  local copies, waits for them, and re-layouts  1.44 us (1%)
    pallas_call x1, Pallas kernels, on_device(): pl.pallas_call(kernel, out_shape=[grid, grid] + [arr((n, 128)) for n in r...  127 us
    pallas_call x1, Pallas kernels, on_device(): pl.pallas_call(widen_kernel, out_shape=[arr((D, 3 * D), F32), arr((D, 3 *...  6.26 us

profile of v3, /device:TPU:1, one launch (start us, length us, event | category | flops | bytes accessed | tf_op | source)
XLA Modules:
  0.0 135.7 jit_solution(16850173645418609884)
XLA Ops:
  0.6 127.3 %window_pair.1 = (bf16[12,12,2,512]{3,2,1,0:T(2,128)(2,1)}, bf16[12,12,2,512]{3,2,1,0:T(2,128)(2,1)}, bf16[8192,128]{1,0:T(8,128)(2,1)}, bf16[6144,128]{1,0:T(8,...) custom-call(bf16[12,12,2,512]{3,2,1,0:T(2,128)(2,1)} %bitcast.17, bf16[12,12,2,512]{3,2,1,0:T(2,128)(2,1)} %bitcast.18, ...), custom_call_target="tpu_custom_call" | custom-call | tf_op jit(solution)/shard_map/window_pair/pallas_call | solution.py:661
  127.9 0.0 copy-start.1
  128.0 0.0 copy-start
  128.0 6.3 %widen_grads.1 = (f32[512,1536]{1,0:T(8,128)}, f32[512,1536]{1,0:T(8,128)}, f32[512,512]{1,0:T(8,128)}, f32[512,512]{1,0:T(8,128)}, f32[1,512]{1,0:T(1,128)}, /*...) custom-call(bf16[16,512,128]{2,1,0:T(8,128)(2,1)} %bitcast.12, bf16[12,512,128]{2,1,0:T(8,128)(2,1)} %bitcast.13, ...), custom_call_target="tpu_custom_call" | custom-call | tf_op jit(solution)/shard_map/widen_grads/pallas_call | solution.py:694
  134.2 0.0 copy-done.1
  134.2 0.7 copy.24
  135.0 0.0 copy-done
  135.0 0.7 copy.25
Async XLA Ops:
  127.9 6.3 %copy-start.1 = (bf16[12,12,2,512]{3,2,1,0:T(2,128)(2,1)S(1)}, bf16[12,12,2,512]{3,2,1,0:T(2,128)(2,1)}, u32[]{:S(2)}) copy-start(bf16[12,12,2,512]{3,2,1,0:T(2,128)(2,1)} %get-tuple-element.24) | copy-start | bytes 884740
  128.0 7.0 %copy-start = (bf16[12,12,2,512]{3,2,1,0:T(2,128)(2,1)S(1)}, bf16[12,12,2,512]{3,2,1,0:T(2,128)(2,1)}, u32[]{:S(2)}) copy-start(bf16[12,12,2,512]{3,2,1,0:T(2,128)(2,1)} %get-tuple-element.25) | copy-start | bytes 884740

commit v4 on v3

--- a/solution.py
+++ b/solution.py
@@ -127,17 +127,7 @@
                 bias[h, rows, lanes] = acc
 
 
-def softmax_head(q, kt, packed, step, high, pen):
-    s = dot(q, kt) * (SCALE * LOG2E)
-    steps = lax.shift_right_logical(packed, 16) if high else packed & 0xFFFF
-    s = s + steps.astype(F32) * step
-    if pen is not None:
-        s = s + pen
-    e = jnp.exp2(s - jnp.max(s, -1, keepdims=True))
-    return e * (1.0 / jnp.sum(e, -1, keepdims=True))
-
-
-def over_heads(p, pt, forward=None, backward=None, groups=(0, 4)):
+def over_heads(p, pt, forward=None, backward=None, groups=(0, 4), wide=2):
     lanes = lax.broadcasted_iota(I32, (WT, 128), 1) // DEPTH
 
     @pl.loop(*groups)
@@ -153,37 +143,52 @@
         if backward is not None:
             dc, dct, a_in, ds_out, dq, dkvt = backward
             dcg = dc[:, pl.ds(g0, 128)]
-        for hh in range(4):
-            h = g * 4 + hh
-            mine = lanes == hh
+        for start in range(0, 4, wide):
+            some = range(start, start + wide)
+            heads = [g * 4 + hh for hh in some]
+            spans = [pl.ds(pl.multiple_of(g0 + hh * DEPTH, DEPTH), DEPTH) for hh in some]
             if forward is not None:
                 bias, steps, high, pen, c, a_out = forward
-                a32 = softmax_head(
-                    jnp.where(mine, qg, zero),
-                    ktg,
-                    bias[h, :, :WT],
-                    steps[pl.ds(h, 1), 0:1],
-                    high,
-                    None if pen is None else pen[...],
-                )
-                a = a32.astype(BF16)
-                ch = dot(a, vg)
-                c_acc = ch if c_acc is None else jnp.where(mine, ch, c_acc)
-                if a_out is not None:
-                    a_out[h] = a
+                s = [dot(jnp.where(lanes == hh, qg, zero), ktg) for hh in some]
+            if backward is not None:
+                da = [dot(jnp.where(lanes == hh, dcg, zero), vtg) for hh in some]
+            if forward is not None:
+                for k, h in enumerate(heads):
+                    packed = bias[h, :, :WT]
+                    entry = lax.shift_right_logical(packed, 16) if high else packed & 0xFFFF
+                    s[k] = s[k] * (SCALE * LOG2E) + entry.astype(F32) * steps[pl.ds(h, 1), 0:1]
+                    if pen is not None:
+                        s[k] = s[k] + pen[...]
+                most = [jnp.max(v, -1, keepdims=True) for v in s]
+                expo = [jnp.exp2(v - m) for v, m in zip(s, most)]
+                total = [1.0 / jnp.sum(v, -1, keepdims=True) for v in expo]
+                a32 = [v * r for v, r in zip(expo, total)]
+                a = [v.astype(BF16) for v in a32]
             else:
-                a = a_in[h]
-                a32 = a.astype(F32)
+                a = [a_in[h] for h in heads]
+                a32 = [v.astype(F32) for v in a]
             if backward is not None:
-                r0 = pl.multiple_of(g0 + hh * DEPTH, DEPTH)
-                da = dot(jnp.where(mine, dcg, zero), vtg)
-                ds = a32 * (da - jnp.sum(a32 * da, -1, keepdims=True))
-                ds_out[:, h, :WT] = ds
-                dsb = ds.astype(BF16)
-                dqh = dot(dsb, kg)
-                q_acc = dqh if q_acc is None else jnp.where(mine, dqh, q_acc)
-                dkvt[pl.ds(r0, DEPTH), :] = (dot(pt[pl.ds(r0, DEPTH), :], dsb) * SCALE).astype(BF16)
-                dkvt[pl.ds(D + r0, DEPTH), :] = dot(dct[pl.ds(r0, DEPTH), :], a).astype(BF16)
+                mean = [jnp.sum(v * w, -1, keepdims=True) for v, w in zip(a32, da)]
+                ds = [v * (w - m) for v, w, m in zip(a32, da, mean)]
+                dsb = [v.astype(BF16) for v in ds]
+            if forward is not None:
+                ctx = [dot(v, vg) for v in a]
+            if backward is not None:
+                dqh = [dot(v, kg) for v in dsb]
+                dk = [dot(pt[span, :], v) * SCALE for span, v in zip(spans, dsb)]
+                dv = [dot(dct[span, :], v) for span, v in zip(spans, a)]
+            for k, hh in enumerate(some):
+                own = lanes == hh
+                if forward is not None:
+                    c_acc = ctx[k] if c_acc is None else jnp.where(own, ctx[k], c_acc)
+                    if a_out is not None:
+                        a_out[heads[k]] = a[k]
+                if backward is not None:
+                    q_acc = dqh[k] if q_acc is None else jnp.where(own, dqh[k], q_acc)
+                    ds_out[:, heads[k], :WT] = ds[k]
+                    at = pl.multiple_of(g0 + hh * DEPTH, DEPTH)
+                    dkvt[pl.ds(at, DEPTH), :] = dk[k].astype(BF16)
+                    dkvt[pl.ds(D + at, DEPTH), :] = dv[k].astype(BF16)
         if forward is not None:
             c[:, pl.ds(g0, 128)] = c_acc.astype(BF16)
         if backward is not None:
@@ -219,9 +224,11 @@
         dst[at : at + D, :] = value[:, n * 128 : (n + 1) * 128].astype(BF16)
 
 
-def qkv_grads(h, dq, dkvt, grads):
-    put_columns(dot_tn(h, dq[...]), grads, 0)
-    put_columns(dot_nt(h.T, dkvt[...]), grads, 4)
+def qkv_grads(h, ht, dq, dkvt, grads, first, last):
+    cols = slice(first * 128, last * 128)
+    put_columns(dot_tn(h, dq[:, cols]), grads, 0)
+    put_columns(dot_nt(ht, dkvt[cols, :]), grads, last - first)
+    put_columns(dot_nt(ht, dkvt[D + first * 128 : D + last * 128, :]), grads, 2 * (last - first))
 
 
 def input_grad(xh, rstd, gain, ef, dq, dkvt, wqkv, g_gain):
@@ -280,7 +287,8 @@
 
 class Job:
     def __init__(self, units, refs, sems, where):
-        self.src, self.out, self.r0, self.a, self.r1, self.b, self.r2, self.c4 = refs
+        self.src, self.out, self.r0, self.r1, self.b, self.r2, self.c4 = refs
+        self.a = self.r0
         self.send, self.recv = sems
         self.half = self.src.shape[0] // 2
         self.where = where
@@ -449,7 +457,7 @@
             self.wait()
 
 
-UNITS = {8192: (6, 5, 5), 6144: (4, 4, 4), 2048: (2, 1, 1)}
+UNITS = {8192: (6, 5, 5), 3072: (2, 2, 2), 2048: (2, 1, 1)}
 
 
 def small_scratch():
@@ -467,7 +475,6 @@
 def job_scratch(rows):
     half = rows // 2
     return [
-        pltpu.VMEM((half, 128), BF16),
         pltpu.VMEM((half, 128), BF16),
         pltpu.VMEM((3, half // 4, 128), BF16),
         pltpu.VMEM((half // 4, 128), BF16),
@@ -493,8 +500,9 @@
 
 
 def kernel(
-    tok_ref, cot_ref, reg_ref, gain1, gain2, wqkv1, wqkv2, wo1, wo2, tab1, tab2, rel_ref,
-    mixed_ref, gt_ref, o2, oq, oo, os,
+    tok_ref, cot_hbm, reg_ref, gain1, gain2, wqkv1_hbm, wqkv2_hbm, wo1_hbm, wo2_hbm, tab1, tab2, rel_ref,
+    mixed_ref, gt_ref, out2, out_a, out_b, out_o, os,
+    cot_ref, wqkv1, wqkv2, wo1, wo2, g2, ga, gb, go, in_sems, out_sems,
     quad, packed, highs, lows, step1, step2, bias, p1, pt1, c1, a1, p2, pt2, c2,
     dc, dct, dq, dkvt, pen, ds1, ds2, their_ds1, their_ds2, y, z, dz, dy,
     small, g_gain1, g_gain2, sums,
@@ -506,12 +514,18 @@
     peers = all_peers(where) + [near(by, m[2], m[3]) for by in (-1, 1) for m in MOVES]
     for dev in peers:
         pl.semaphore_signal(barrier, inc=1, device_id=dev, device_id_type=MESH)
+    brought = []
+    for n, (src, dst) in enumerate(
+        ((wqkv1_hbm, wqkv1), (wo1_hbm, wo1), (cot_hbm, cot_ref), (wo2_hbm, wo2), (wqkv2_hbm, wqkv2))
+    ):
+        brought.append(pltpu.make_async_copy(src, dst, in_sems.at[n]))
+        brought[-1].start()
     jobs = []
-    for n, ref in enumerate((o2, oq, oo)):
-        held = job_mem[n * 8 : n * 8 + 8]
-        jobs.append(Job(UNITS[ref.shape[0]], (ref, ref) + held[:6], held[6:], where))
-    sum2, sum_q, sum_o = (job.stage for job in jobs)
-    held = job_mem[24:]
+    for n, ref in enumerate((g2, ga, gb, go)):
+        held = job_mem[n * 7 : n * 7 + 7]
+        jobs.append(Job(UNITS[ref.shape[0]], (ref, ref) + held[:5], held[5:], where))
+    sum2, sum_a, sum_b, sum_o = (job.stage for job in jobs)
+    held = job_mem[28:]
     sum_s = SmallJob((small, os) + held[:4], held[4:], where).stage
 
     def to_pair(n, src, dst):
@@ -521,6 +535,12 @@
         )
         copy.start()
         return copy
+
+    written = []
+
+    def write(n, src, dst):
+        written.append(pltpu.make_async_copy(src, dst, out_sems.at[n]))
+        written[-1].start()
 
     mine = pl.multiple_of(core * 144, 16)
     theirs = pl.multiple_of((1 - core) * 144, 16)
@@ -535,6 +555,8 @@
         rows = pl.ds(pl.multiple_of(mine + part * 48, 16), 48)
         sent.append(to_pair(part, bias.at[:, rows], bias.at[:, rows]))
 
+    for copy in brought[:2]:
+        copy.wait()
     into_quads(tok_ref, quad)
     x = quad[...]
     xh, _ = norm(x)
@@ -545,6 +567,8 @@
     put_quads((x + dot(c1[...], wo1[...])).astype(BF16), y)
 
     on = shift(-1, y, z, send_on, recv_on)
+    for copy in brought[2:]:
+        copy.wait()
     into_quads(cot_ref, quad)
     ef = quad[...]
     e = ef.astype(BF16)
@@ -567,8 +591,8 @@
     put_quads(input_grad(xh, rstd, gain2[...], ef, dq, dkvt, wqkv2, g_gain2).astype(BF16), dz)
     back = shift(1, dz, dy, send_back, recv_back)
     ds_sent = [to_pair(3, ds2.at[pl.ds(theirs, 144)], their_ds2)]
-    qkv_grads(h, dq, dkvt, o2)
-    put_columns(dot_tn(c2[...], e), o2, 12)
+    qkv_grads(h, h.T, dq, dkvt, g2, 0, 4)
+    put_columns(dot_tn(c2[...], e), g2, 12)
     sum2(0)
     quad[...] = x + dot(c2[...], wo2[...])
     out_of_quads(quad, mixed_ref)
@@ -580,55 +604,71 @@
         copy.wait()
     ef = get_quads(dy)
     e = ef.astype(BF16)
-    put_columns(dot_tn(c1[...], e), oo, 0)
+    put_columns(dot_tn(c1[...], e), go, 0)
     sum2(1)
     sum_o(0)
+    ht = h.T
     context_grad(e, wo1, dc, dct)
     sum_o(1)
     over_heads(p1, pt1, None, (dc, dct, a1, ds1, dq, dkvt), (0, 2))
+    ds_sent.append(to_pair(4, ds1.at[pl.ds(theirs, 144), pl.ds(0, 8)], their_ds1.at[:, pl.ds(0, 8)]))
+    qkv_grads(h, ht, dq, dkvt, ga, 0, 2)
+    sum_a(0)
     sum2(2)
+    over_heads(p1, pt1, None, (dc, dct, a1, ds1, dq, dkvt), (2, 4))
+    ds_sent.append(to_pair(5, ds1.at[pl.ds(theirs, 144), pl.ds(8, 8)], their_ds1.at[:, pl.ds(8, 8)]))
+    sum_a(1)
+    qkv_grads(h, ht, dq, dkvt, gb, 2, 4)
+    sum_b(0)
     sum_o(2)
-    over_heads(p1, pt1, None, (dc, dct, a1, ds1, dq, dkvt), (2, 4))
-    ds_sent.append(to_pair(4, ds1.at[pl.ds(theirs, 144)], their_ds1))
+    quad[...] = input_grad(xh, rstd, gain1[...], ef, dq, dkvt, wqkv1, g_gain1)
+    sum_b(1)
     sum2(3)
-    sum_o(3)
-    qkv_grads(h, dq, dkvt, oq)
-    sum_q(0)
-    sum2(4)
-    sum_o(4)
-    quad[...] = input_grad(xh, rstd, gain1[...], ef, dq, dkvt, wqkv1, g_gain1)
-    sum_q(1)
-    sum2(5)
-    out_of_quads(quad, gt_ref)
-    sum_o(5)
     for copy in ds_sent:
         copy.wait()
 
     blocks = ((ds1, their_ds1), (ds2, their_ds2))
-    for part in range(3):
-        table_grads(blocks, highs, lows, sums, first, part * 6, part * 6 + 6)
-        sum_q(2 + part)
-        if part > 0:
-            sum2(5 + part)
-            sum_o(5 + part)
+    between = (
+        ((sum_a, 2), (sum_o, 3), (sum2, 4)),
+        ((sum_b, 2), (sum_a, 3), (sum2, 5)),
+        ((sum_b, 3), (sum_o, 4), (sum_a, 4)),
+        ((sum_b, 4), (sum_o, 5), (sum_a, 5)),
+        ((sum_b, 5), (sum2, 6), (sum_o, 6)),
+        ((sum_a, 6), (sum2, 7), (sum_o, 7)),
+    )
+    for part, steps in enumerate(between):
+        table_grads(blocks, highs, lows, sums, first, part * 3, part * 3 + 3)
+        for step, n in steps:
+            step(n)
     small[:224, :] = sums[:, :128].astype(BF16)
     small[224:448, :] = sums[:, 128:].astype(BF16)
     gains = [g[:, n * 128 : (n + 1) * 128] for g in (g_gain1, g_gain2) for n in range(4)]
     gains.append(jnp.zeros((SROWS - 456, 128), F32))
     small[448:, :] = jnp.concatenate(gains, 0).astype(BF16)
     sum_s(0)
+    write(0, g2, out2)
+    write(1, go, out_o)
     sum_s(1)
-    sum_q(5)
+    out_of_quads(quad, gt_ref)
     sum_s(2)
+    sum_b(6)
+    sum_a(7)
+    write(2, ga, out_a)
     sum_s(3)
-    sum_q(6)
+    sum_b(7)
+    write(3, gb, out_b)
     sum_s(4)
     sum_s(5)
-    sum_q(7)
-
-
-def widen_kernel(s2, sq, so, small, gq1, gq2, gp1, gp2, gg1, gg2, gt1, gt2):
-    for src, at, dst in ((sq, 0, gq1), (so, 0, gp1), (s2, 0, gq2), (s2, 12, gp2)):
+    for copy in written:
+        copy.wait()
+
+
+def widen_kernel(s2, sa, sb, so, small, gq1, gq2, gp1, gp2, gg1, gg2, gt1, gt2):
+    for k in range(3):
+        for n in range(4):
+            src = sa if n < 2 else sb
+            gq1[:, (k * 4 + n) * 128 : (k * 4 + n + 1) * 128] = src[k * 2 + n % 2].astype(F32)
+    for src, at, dst in ((so, 0, gp1), (s2, 0, gq2), (s2, 12, gp2)):
         for n in range(dst.shape[1] // 128):
             dst[:, n * 128 : (n + 1) * 128] = src[at + n].astype(F32)
 
@@ -655,15 +695,18 @@
         return pltpu.VMEM(shape, dtype)
 
     grid = arr((12, 12, 2, D))
-    rows = (8192, 6144, 2048)
+    rows = (8192, 3072, 3072, 2048)
+    hbm = pl.BlockSpec(memory_space=pl.ANY)
+    weights = [mem(D, 3 * D), mem(D, 3 * D), mem(D, D), mem(D, D)]
     three = pltpu.SemaphoreType.DMA((3,))
-    five = pltpu.SemaphoreType.DMA((5,))
-    mixed, grad_tokens, s2, sq, so, small = pl.pallas_call(
+    six = pltpu.SemaphoreType.DMA((6,))
+    mixed, grad_tokens, s2, sa, sb, so, small = pl.pallas_call(
         kernel,
         out_shape=[grid, grid] + [arr((n, 128)) for n in rows] + [arr((SROWS, 128))],
-        in_specs=[VM, VM, SM] + [VM] * 9,
-        out_specs=[VM] * 6,
-        scratch_shapes=[
+        in_specs=[VM, hbm, SM, VM, VM] + [hbm] * 4 + [VM] * 3,
+        out_specs=[VM, VM] + [hbm] * 4 + [VM],
+        scratch_shapes=[mem(12, 12, 2, D)] + weights + [mem(n, 128) for n in rows] + [six, six]
+        + [
             mem(WT, D, dtype=F32), mem(HEADS, CHUNKS * 128, dtype=I32),
             mem(WT, PADW, dtype=I32), mem(WT, PADW, dtype=I32), mem(HEADS, 128, dtype=F32), mem(HEADS, 128, dtype=F32),
             mem(HEADS, WT, PADW, dtype=I32),
@@ -675,7 +718,7 @@
         ]
         + [mem(4, QPAD, D)] * 4
         + [mem(SROWS, 128), mem(1, D, dtype=F32), mem(1, D, dtype=F32), mem(224, 256, dtype=F32)]
-        + [three] * 4 + [five] * 2
+        + [three] * 4 + [six] * 2
         + [ref for n in rows for ref in job_scratch(n)] + small_scratch(),
         compiler_params=pltpu.CompilerParams(vmem_limit_bytes=62 << 20, collective_id=3, has_side_effects=True),
         name="window_pair",
@@ -697,15 +740,15 @@
             arr((D, 3 * D), F32), arr((D, 3 * D), F32), arr((D, D), F32), arr((D, D), F32),
             arr((1, D), F32), arr((1, D), F32), arr((HEADS, NB), F32), arr((HEADS, NB), F32),
         ],
-        grid=(4,),
-        in_specs=[part(16, 128, 128), part(12, 128, 128), part(4, 128, 128), whole(SROWS, 128)],
+        grid=(8,),
+        in_specs=[part(16, 64, 128), part(6, 64, 128), part(6, 64, 128), part(4, 64, 128), whole(SROWS, 128)],
         out_specs=[
-            part(128, 3 * D), part(128, 3 * D), part(128, D), part(128, D),
+            part(64, 3 * D), part(64, 3 * D), part(64, D), part(64, D),
             whole(1, D), whole(1, D), whole(HEADS, NB), whole(HEADS, NB),
         ],
         compiler_params=PARAMS,
         name="widen_grads",
-    )(s2.reshape(16, D, 128), sq.reshape(12, D, 128), so.reshape(4, D, 128), small)
+    )(s2.reshape(16, D, 128), sa.reshape(6, D, 128), sb.reshape(6, D, 128), so.reshape(4, D, 128), small)
     mixed, grad_tokens = mixed.transpose(2, 0, 1, 3), grad_tokens.transpose(2, 0, 1, 3)
     return mixed, grad_tokens, gg1.reshape(D), gg2.reshape(D), gq1, gq2, gp1, gp2, gt1, gt2
 

time: 136 us -> 132 us (0.971)
  Pallas kernels: 134 us -> 129 us
    pallas_call x1, Pallas kernels: 127 us -> 122 us  [on_device(): pl.pallas_call(kernel, out_shape=[grid, grid] + [arr((n, 128)) for n in r...]
    pallas_call x1, Pallas kernels: 6.26 us -> 7.63 us  [on_device(): pl.pallas_call(widen_kernel, out_shape=[arr((D, 3 * D), F32), arr((D, 3 *...]
where the time goes in v4:
time: 132 us; the launch traced here: 131 us
  Pallas kernels  129 us (98%)
  local copies, waits for them, and re-layouts  1.44 us (1%)
    pallas_call x1, Pallas kernels, on_device(): pl.pallas_call(kernel, out_shape=[grid, grid] + [arr((n, 128)) for n in r...  122 us
    pallas_call x1, Pallas kernels, on_device(): pl.pallas_call(widen_kernel, out_shape=[arr((D, 3 * D), F32), arr((D, 3 *...  7.63 us

profile of v4, /device:TPU:1, one launch (start us, length us, event | category | flops | bytes accessed | tf_op | source)
XLA Modules:
  0.0 131.4 jit_solution(16073442786351864105)
XLA Ops:
  0.6 121.6 %window_pair.1 = (bf16[12,12,2,512]{3,2,1,0:T(2,128)(2,1)}, bf16[12,12,2,512]{3,2,1,0:T(2,128)(2,1)}, bf16[8192,128]{1,0:T(8,128)(2,1)}, bf16[3072,128]{1,0:T(8,...) custom-call(bf16[12,12,2,512]{3,2,1,0:T(2,128)(2,1)} %bitcast.19, ...), custom_call_target="tpu_custom_call" | custom-call | tf_op jit(solution)/shard_map/window_pair/pallas_call | solution.py:703
  122.3 0.0 copy-start.1
  122.3 0.0 copy-start
  122.3 7.6 %widen_grads.1 = (f32[512,1536]{1,0:T(8,128)}, f32[512,1536]{1,0:T(8,128)}, f32[512,512]{1,0:T(8,128)}, f32[512,512]{1,0:T(8,128)}, f32[1,512]{1,0:T(1,128)}, /*...) custom-call(bf16[16,512,128]{2,1,0:T(8,128)(2,1)} %bitcast.13, bf16[6,512,128]{2,1,0:T(8,128)(2,1)} %bitcast.14, ...), custom_call_target="tpu_custom_call" | custom-call | tf_op jit(solution)/shard_map/widen_grads/pallas_call | solution.py:737
  129.9 0.0 copy-done.1
  130.0 0.7 copy.24
  130.7 0.0 copy-done
  130.7 0.7 copy.25
Async XLA Ops:
  122.3 7.7 %copy-start.1 = (bf16[12,12,2,512]{3,2,1,0:T(2,128)(2,1)S(1)}, bf16[12,12,2,512]{3,2,1,0:T(2,128)(2,1)}, u32[]{:S(2)}) copy-start(bf16[12,12,2,512]{3,2,1,0:T(2,128)(2,1)} %get-tuple-element.25) | copy-start | bytes 884740
  122.3 8.4 %copy-start = (bf16[12,12,2,512]{3,2,1,0:T(2,128)(2,1)S(1)}, bf16[12,12,2,512]{3,2,1,0:T(2,128)(2,1)}, u32[]{:S(2)}) copy-start(bf16[12,12,2,512]{3,2,1,0:T(2,128)(2,1)} %get-tuple-element.26) | copy-start | bytes 884740

commit v5 on v4

--- a/solution.py
+++ b/solution.py
@@ -211,7 +211,7 @@
                 low = jnp.broadcast_to(low8[i : i + 1], (256, PADW))
                 picked = []
                 for block, theirs in blocks:
-                    ds = (block[r * 8 + i] + theirs[(r - first) * 8 + i]).astype(BF16)
+                    ds = (block[r * 8 + i] + theirs[(r - first) * 8 + i].astype(F32)).astype(BF16)
                     picked += [jnp.where(high == jnp.array(k, BF16), ds, jnp.zeros_like(ds)) for k in range(HIGHS)]
                 left.append(jnp.concatenate(picked, 0))
                 right.append(jnp.where(low == low_of, one, nil))
@@ -504,7 +504,7 @@
     mixed_ref, gt_ref, out2, out_a, out_b, out_o, os,
     cot_ref, wqkv1, wqkv2, wo1, wo2, g2, ga, gb, go, in_sems, out_sems,
     quad, packed, highs, lows, step1, step2, bias, p1, pt1, c1, a1, p2, pt2, c2,
-    dc, dct, dq, dkvt, pen, ds1, ds2, their_ds1, their_ds2, y, z, dz, dy,
+    dc, dct, dq, dkvt, pen, ds1, ds2, their_ds1, their_ds2, ds1_out, ds2_out, y, z, dz, dy,
     small, g_gain1, g_gain2, sums,
     send_on, recv_on, send_back, recv_back, pair_send, pair_recv, *job_mem,
 ):
@@ -542,6 +542,13 @@
         written.append(pltpu.make_async_copy(src, dst, out_sems.at[n]))
         written[-1].start()
 
+    def ds_to_pair(n, ds, out, dst):
+        @pl.loop(0, 18)
+        def _(r):
+            out[pl.ds(r * 8, 8)] = ds[pl.ds(theirs + r * 8, 8)].astype(BF16)
+
+        return to_pair(n, out, dst)
+
     mine = pl.multiple_of(core * 144, 16)
     theirs = pl.multiple_of((1 - core) * 144, 16)
     first = core * 18
@@ -590,51 +597,49 @@
     over_heads(p2, pt2, (bias, step2, False, pen, c2, None), (dc, dct, None, ds2, dq, dkvt))
     put_quads(input_grad(xh, rstd, gain2[...], ef, dq, dkvt, wqkv2, g_gain2).astype(BF16), dz)
     back = shift(1, dz, dy, send_back, recv_back)
-    ds_sent = [to_pair(3, ds2.at[pl.ds(theirs, 144)], their_ds2)]
     qkv_grads(h, h.T, dq, dkvt, g2, 0, 4)
     put_columns(dot_tn(c2[...], e), g2, 12)
     sum2(0)
     quad[...] = x + dot(c2[...], wo2[...])
     out_of_quads(quad, mixed_ref)
+    ds_sent = [ds_to_pair(3, ds2, ds2_out, their_ds2)]
 
     into_quads(tok_ref, quad)
     xh, rstd = norm(quad[...])
     h = (xh * gain1[...]).astype(BF16)
+    ht = h.T
+    sum2(1)
     for copy in back:
         copy.wait()
     ef = get_quads(dy)
     e = ef.astype(BF16)
     put_columns(dot_tn(c1[...], e), go, 0)
-    sum2(1)
     sum_o(0)
-    ht = h.T
     context_grad(e, wo1, dc, dct)
+    over_heads(p1, pt1, None, (dc, dct, a1, ds1, dq, dkvt), (0, 2))
     sum_o(1)
-    over_heads(p1, pt1, None, (dc, dct, a1, ds1, dq, dkvt), (0, 2))
-    ds_sent.append(to_pair(4, ds1.at[pl.ds(theirs, 144), pl.ds(0, 8)], their_ds1.at[:, pl.ds(0, 8)]))
     qkv_grads(h, ht, dq, dkvt, ga, 0, 2)
     sum_a(0)
+    over_heads(p1, pt1, None, (dc, dct, a1, ds1, dq, dkvt), (2, 4))
+    ds_sent.append(ds_to_pair(4, ds1, ds1_out, their_ds1))
     sum2(2)
-    over_heads(p1, pt1, None, (dc, dct, a1, ds1, dq, dkvt), (2, 4))
-    ds_sent.append(to_pair(5, ds1.at[pl.ds(theirs, 144), pl.ds(8, 8)], their_ds1.at[:, pl.ds(8, 8)]))
     sum_a(1)
     qkv_grads(h, ht, dq, dkvt, gb, 2, 4)
     sum_b(0)
+    quad[...] = input_grad(xh, rstd, gain1[...], ef, dq, dkvt, wqkv1, g_gain1)
     sum_o(2)
-    quad[...] = input_grad(xh, rstd, gain1[...], ef, dq, dkvt, wqkv1, g_gain1)
-    sum_b(1)
-    sum2(3)
     for copy in ds_sent:
         copy.wait()
+    sum_b(1)
 
     blocks = ((ds1, their_ds1), (ds2, their_ds2))
     between = (
-        ((sum_a, 2), (sum_o, 3), (sum2, 4)),
-        ((sum_b, 2), (sum_a, 3), (sum2, 5)),
-        ((sum_b, 3), (sum_o, 4), (sum_a, 4)),
+        ((sum2, 3), (sum_a, 2)),
+        ((sum_o, 3), (sum_b, 2), (sum2, 4)),
+        ((sum_a, 3), (sum_b, 3)),
+        ((sum2, 5), (sum_o, 4), (sum_a, 4)),
         ((sum_b, 4), (sum_o, 5), (sum_a, 5)),
-        ((sum_b, 5), (sum2, 6), (sum_o, 6)),
-        ((sum_a, 6), (sum2, 7), (sum_o, 7)),
+        ((sum_b, 5),),
     )
     for part, steps in enumerate(between):
         table_grads(blocks, highs, lows, sums, first, part * 3, part * 3 + 3)
@@ -646,15 +651,20 @@
     gains.append(jnp.zeros((SROWS - 456, 128), F32))
     small[448:, :] = jnp.concatenate(gains, 0).astype(BF16)
     sum_s(0)
-    write(0, g2, out2)
-    write(1, go, out_o)
+    sum2(6)
     sum_s(1)
     out_of_quads(quad, gt_ref)
+    sum_o(6)
+    sum_a(6)
     sum_s(2)
     sum_b(6)
+    sum2(7)
+    write(0, g2, out2)
+    sum_o(7)
+    write(1, go, out_o)
+    sum_s(3)
     sum_a(7)
     write(2, ga, out_a)
-    sum_s(3)
     sum_b(7)
     write(3, gb, out_b)
     sum_s(4)
@@ -663,25 +673,38 @@
         copy.wait()
 
 
-def widen_kernel(s2, sa, sb, so, small, gq1, gq2, gp1, gp2, gg1, gg2, gt1, gt2):
-    for k in range(3):
+def widen_kernel(s2, sa, sb, so, small, gq1, gq2, gp1, gp2, gg1, gg2, gt1, gt2, m2, ma, mb, mo, wide, in_sems, out_sems):
+    ins = [pltpu.make_async_copy(so, mo, in_sems.at[0])]
+    ins += [pltpu.make_async_copy(s2.at[pl.ds(k * 4, 4)], m2.at[pl.ds(k * 4, 4)], in_sems.at[1 + k]) for k in range(4)]
+    ins += [pltpu.make_async_copy(sa, ma, in_sems.at[5]), pltpu.make_async_copy(sb, mb, in_sems.at[6])]
+    for copy in ins:
+        copy.start()
+
+    def slab(dst, k):
+        return dst.at[:, pl.ds(k * D, D)]
+
+    plan = [(mo, 0, gp1, 1)] + [(m2, k * 4, slab(gq2, k), 1) for k in range(3)] + [(m2, 12, gp2, 1)]
+    plan += [(None, k, slab(gq1, k), 2 if k == 0 else 0) for k in range(3)]
+    outs = []
+    waits = iter(ins)
+    for n, (src, at, dst, arrivals) in enumerate(plan):
+        for _ in range(arrivals):
+            next(waits).wait()
+        for c in range(4):
+            block = src[at + c] if src is not None else (ma if c < 2 else mb)[at * 2 + c % 2]
+            wide[n, :, c * 128 : (c + 1) * 128] = block.astype(F32)
+        outs.append(pltpu.make_async_copy(wide.at[n], dst, out_sems.at[n]))
+        outs[-1].start()
+    tail = small[448:464, :].astype(F32)
+    for b, (gg, gt) in enumerate(((gg1, gt1), (gg2, gt2))):
         for n in range(4):
-            src = sa if n < 2 else sb
-            gq1[:, (k * 4 + n) * 128 : (k * 4 + n + 1) * 128] = src[k * 2 + n % 2].astype(F32)
-    for src, at, dst in ((so, 0, gp1), (s2, 0, gq2), (s2, 12, gp2)):
-        for n in range(dst.shape[1] // 128):
-            dst[:, n * 128 : (n + 1) * 128] = src[at + n].astype(F32)
-
-    @pl.when(pl.program_id(0) == 0)
-    def _():
-        tail = small[448:464, :].astype(F32)
-        for b, (gg, gt) in enumerate(((gg1, gt1), (gg2, gt2))):
-            for n in range(4):
-                gg[:, n * 128 : (n + 1) * 128] = tail[b * 4 + n : b * 4 + n + 1]
-            for k in range(CHUNKS):
-                at = (b * HIGHS + k // 2) * 16 + (k % 2) * 224
-                width = min(128, NB - k * 128)
-                gt[:, k * 128 : k * 128 + width] = small[at : at + 16, :width].astype(F32)
+            gg[:, n * 128 : (n + 1) * 128] = tail[b * 4 + n : b * 4 + n + 1]
+        for k in range(CHUNKS):
+            at = (b * HIGHS + k // 2) * 16 + (k % 2) * 224
+            width = min(128, NB - k * 128)
+            gt[:, k * 128 : k * 128 + width] = small[at : at + 16, :width].astype(F32)
+    for copy in outs:
+        copy.wait()
 
 
 def on_device(
@@ -714,7 +737,7 @@
             mem(WT, 3 * D), mem(3 * D, WT), mem(WT, D),
             mem(WT, D), mem(D, WT), mem(WT, D), mem(2 * D, WT), mem(WT, WT, dtype=F32),
             mem(WT, HEADS, PADW, dtype=F32), mem(WT, HEADS, PADW, dtype=F32),
-            mem(144, HEADS, PADW, dtype=F32), mem(144, HEADS, PADW, dtype=F32),
+            mem(144, HEADS, PADW), mem(144, HEADS, PADW), mem(144, HEADS, PADW), mem(144, HEADS, PADW),
         ]
         + [mem(4, QPAD, D)] * 4
         + [mem(SROWS, 128), mem(1, D, dtype=F32), mem(1, D, dtype=F32), mem(224, 256, dtype=F32)]
@@ -728,23 +751,17 @@
         proj_first, proj_second, table_first, table_second, rel_index,
     )
 
-    def part(*shape):
-        return pl.BlockSpec(shape, lambda i: (0, i, 0) if len(shape) == 3 else (i, 0))
-
-    def whole(*shape):
-        return pl.BlockSpec(shape, lambda i: (0, 0))
-
     gq1, gq2, gp1, gp2, gg1, gg2, gt1, gt2 = pl.pallas_call(
         widen_kernel,
         out_shape=[
             arr((D, 3 * D), F32), arr((D, 3 * D), F32), arr((D, D), F32), arr((D, D), F32),
             arr((1, D), F32), arr((1, D), F32), arr((HEADS, NB), F32), arr((HEADS, NB), F32),
         ],
-        grid=(8,),
-        in_specs=[part(16, 64, 128), part(6, 64, 128), part(6, 64, 128), part(4, 64, 128), whole(SROWS, 128)],
-        out_specs=[
-            part(64, 3 * D), part(64, 3 * D), part(64, D), part(64, D),
-            whole(1, D), whole(1, D), whole(HEADS, NB), whole(HEADS, NB),
+        in_specs=[hbm] * 4 + [VM],
+        out_specs=[hbm] * 4 + [VM] * 4,
+        scratch_shapes=[
+            mem(16, D, 128), mem(6, D, 128), mem(6, D, 128), mem(4, D, 128), mem(8, D, D, dtype=F32),
+            pltpu.SemaphoreType.DMA((7,)), pltpu.SemaphoreType.DMA((8,)),
         ],
         compiler_params=PARAMS,
         name="widen_grads",

time: 132 us -> 125 us (0.947)
  Pallas kernels: 129 us -> 122 us
    pallas_call x1, Pallas kernels: 122 us -> 116 us  [on_device(): pl.pallas_call(kernel, out_shape=[grid, grid] + [arr((n, 128)) for n in r...]
    pallas_call x1, Pallas kernels: 7.63 us -> 6.25 us  [on_device(): pl.pallas_call(widen_kernel, out_shape=[arr((D, 3 * D), F32), arr((D, 3 *...]
where the time goes in v5:
time: 125 us
  Pallas kernels  122 us (98%)
  local copies, waits for them, and re-layouts  1.44 us (1%)
    pallas_call x1, Pallas kernels, on_device(): pl.pallas_call(kernel, out_shape=[grid, grid] + [arr((n, 128)) for n in r...  116 us
    pallas_call x1, Pallas kernels, on_device(): pl.pallas_call(widen_kernel, out_shape=[arr((D, 3 * D), F32), arr((D, 3 *...  6.25 us

profile of v5, /device:TPU:1, one launch (start us, length us, event | category | flops | bytes accessed | tf_op | source)
XLA Modules:
  0.0 124.5 jit_solution(7293031074482851601)
XLA Ops:
  0.6 116.2 %window_pair.1 = (bf16[12,12,2,512]{3,2,1,0:T(2,128)(2,1)}, bf16[12,12,2,512]{3,2,1,0:T(2,128)(2,1)}, bf16[8192,128]{1,0:T(8,128)(2,1)}, bf16[3072,128]{1,0:T(8,...) custom-call(bf16[12,12,2,512]{3,2,1,0:T(2,128)(2,1)} %bitcast.19, ...), custom_call_target="tpu_custom_call" | custom-call | tf_op jit(solution)/shard_map/window_pair/pallas_call | solution.py:726
  116.8 0.0 copy-start.1
  116.8 0.0 copy-start
  116.8 6.3 %widen_grads.1 = (f32[512,1536]{1,0:T(8,128)}, f32[512,1536]{1,0:T(8,128)}, f32[512,512]{1,0:T(8,128)}, f32[512,512]{1,0:T(8,128)}, f32[1,512]{1,0:T(1,128)}, /*...) custom-call(bf16[16,512,128]{2,1,0:T(8,128)(2,1)} %bitcast.13, bf16[6,512,128]{2,1,0:T(8,128)(2,1)} %bitcast.14, ...), custom_call_target="tpu_custom_call" | custom-call | tf_op jit(solution)/shard_map/widen_grads/pallas_call | solution.py:754
  123.1 0.0 copy-done.1
  123.1 0.7 copy.24
  123.8 0.0 copy-done
  123.8 0.7 copy.25
Async XLA Ops:
  116.8 6.3 %copy-start.1 = (bf16[12,12,2,512]{3,2,1,0:T(2,128)(2,1)S(1)}, bf16[12,12,2,512]{3,2,1,0:T(2,128)(2,1)}, u32[]{:S(2)}) copy-start(bf16[12,12,2,512]{3,2,1,0:T(2,128)(2,1)} %get-tuple-element.25) | copy-start | bytes 884740
  116.8 7.0 %copy-start = (bf16[12,12,2,512]{3,2,1,0:T(2,128)(2,1)S(1)}, bf16[12,12,2,512]{3,2,1,0:T(2,128)(2,1)}, u32[]{:S(2)}) copy-start(bf16[12,12,2,512]{3,2,1,0:T(2,128)(2,1)} %get-tuple-element.26) | copy-start | bytes 884740

commit v6 on v5

--- a/solution.py
+++ b/solution.py
@@ -570,7 +570,7 @@
     project((xh * gain1[...]).astype(BF16), wqkv1, p1, pt1)
     for copy in sent:
         copy.wait()
-    over_heads(p1, pt1, forward=(bias, step1, True, None, c1, a1))
+    over_heads(p1, pt1, forward=(bias, step1, True, None, c1, a1), wide=4)
     put_quads((x + dot(c1[...], wo1[...])).astype(BF16), y)
 
     on = shift(-1, y, z, send_on, recv_on)
@@ -616,11 +616,11 @@
     put_columns(dot_tn(c1[...], e), go, 0)
     sum_o(0)
     context_grad(e, wo1, dc, dct)
-    over_heads(p1, pt1, None, (dc, dct, a1, ds1, dq, dkvt), (0, 2))
+    over_heads(p1, pt1, None, (dc, dct, a1, ds1, dq, dkvt), (0, 2), 4)
     sum_o(1)
     qkv_grads(h, ht, dq, dkvt, ga, 0, 2)
     sum_a(0)
-    over_heads(p1, pt1, None, (dc, dct, a1, ds1, dq, dkvt), (2, 4))
+    over_heads(p1, pt1, None, (dc, dct, a1, ds1, dq, dkvt), (2, 4), 4)
     ds_sent.append(ds_to_pair(4, ds1, ds1_out, their_ds1))
     sum2(2)
     sum_a(1)

time: 125 us -> 124 us (level)
  no operation moved by 1% of the time
where the time goes in v6:
time: 124 us
  Pallas kernels  122 us (98%)
  local copies, waits for them, and re-layouts  1.44 us (1%)
    pallas_call x1, Pallas kernels, on_device(): pl.pallas_call(kernel, out_shape=[grid, grid] + [arr((n, 128)) for n in r...  116 us
    pallas_call x1, Pallas kernels, on_device(): pl.pallas_call(widen_kernel, out_shape=[arr((D, 3 * D), F32), arr((D, 3 *...  6.25 us

profile of v6, /device:TPU:1, one launch (start us, length us, event | category | flops | bytes accessed | tf_op | source)
XLA Modules:
  0.0 123.9 jit_solution(5173299487387560788)
XLA Ops:
  0.6 115.5 %window_pair.1 = (bf16[12,12,2,512]{3,2,1,0:T(2,128)(2,1)}, bf16[12,12,2,512]{3,2,1,0:T(2,128)(2,1)}, bf16[8192,128]{1,0:T(8,128)(2,1)}, bf16[3072,128]{1,0:T(8,...) custom-call(bf16[12,12,2,512]{3,2,1,0:T(2,128)(2,1)} %bitcast.19, ...), custom_call_target="tpu_custom_call" | custom-call | tf_op jit(solution)/shard_map/window_pair/pallas_call | solution.py:726
  116.2 0.0 copy-start.1
  116.2 0.0 copy-start
  116.2 6.3 %widen_grads.1 = (f32[512,1536]{1,0:T(8,128)}, f32[512,1536]{1,0:T(8,128)}, f32[512,512]{1,0:T(8,128)}, f32[512,512]{1,0:T(8,128)}, f32[1,512]{1,0:T(1,128)}, /*...) custom-call(bf16[16,512,128]{2,1,0:T(8,128)(2,1)} %bitcast.13, bf16[6,512,128]{2,1,0:T(8,128)(2,1)} %bitcast.14, ...), custom_call_target="tpu_custom_call" | custom-call | tf_op jit(solution)/shard_map/widen_grads/pallas_call | solution.py:754
  122.5 0.0 copy-done.1
  122.5 0.7 copy.24
  123.2 0.0 copy-done
  123.2 0.7 copy.25
Async XLA Ops:
  116.2 6.3 %copy-start.1 = (bf16[12,12,2,512]{3,2,1,0:T(2,128)(2,1)S(1)}, bf16[12,12,2,512]{3,2,1,0:T(2,128)(2,1)}, u32[]{:S(2)}) copy-start(bf16[12,12,2,512]{3,2,1,0:T(2,128)(2,1)} %get-tuple-element.25) | copy-start | bytes 884740
  116.2 7.0 %copy-start = (bf16[12,12,2,512]{3,2,1,0:T(2,128)(2,1)S(1)}, bf16[12,12,2,512]{3,2,1,0:T(2,128)(2,1)}, u32[]{:S(2)}) copy-start(bf16[12,12,2,512]{3,2,1,0:T(2,128)(2,1)} %get-tuple-element.26) | copy-start | bytes 884740
